TPU v7x, 32 devices: a whole 2x2x4 slice. The times are simulated.
32 devices in a mesh: dp: 16 (over z, x, core), tensor: 2 (over y).
Axes of the slice: x: 2, y: 2, z: 4, core: 2. Of those that a mesh axis runs over, the one named last changes fastest.
Arguments:
- tokens: bfloat16 [512, 64, 768], P('tensor', 'dp'), may hold values from -6 to 6
- lengths: int32 [64], P('dp'), may hold values from 64 to 512, as said below
- w_qkv: bfloat16 [3, 768, 768], P(None, 'dp', 'tensor'), may hold values from -0.21875 to 0.21875
- qkv_bias: bfloat16 [2, 768], P(None, ('tensor', 'dp')), may hold values from -3 to 3
- w_out: bfloat16 [768, 768], P('tensor', 'dp'), may hold values from -0.875 to 0.875
- w_in: bfloat16 [768, 3072], P('dp', 'tensor'), may hold values from -0.21875 to 0.21875
- b_in: bfloat16 [3072], P(('tensor', 'dp')), may hold values from -3 to 3
- w_down: bfloat16 [3072, 768], P('tensor', 'dp'), may hold values from -0.109375 to 0.109375
- norm_gains: bfloat16 [2, 768], P(None, ('tensor', 'dp')), may hold values from 0.5 to 1.5
- row_biases: bfloat16 [4, 768], P(None, ('tensor', 'dp')), may hold values from -2 to 2
- cotangent: bfloat16 [512, 64, 768], P('tensor', 'dp'), may hold values from -6 to 6
Outputs:
- out: bfloat16 [512, 64, 768], P('tensor', 'dp')
- d_tokens: float32 [512, 64, 768], P('tensor', 'dp')
- grad_qkv: float32 [3, 768, 768], P(None, 'dp', 'tensor')
- grad_qkv_bias: float32 [2, 768], P(None, ('tensor', 'dp'))
- grad_out: float32 [768, 768], P('tensor', 'dp')
- grad_in: float32 [768, 3072], P('dp', 'tensor')
- grad_in_bias: float32 [3072], P(('tensor', 'dp'))
- grad_down: float32 [3072, 768], P('tensor', 'dp')
- grad_gains: float32 [2, 768], P(None, ('tensor', 'dp'))
- grad_biases: float32 [4, 768], P(None, ('tensor', 'dp'))
Inputs may be any that keep to these rules, and one draw needn't show every extreme that they name: `lengths`: each aligned run of 4 sequences holds at least one sequence of length 512; which one is drawn.
All inputs are finite; a program needn't handle non-finite values.
Results may differ from a plain program's by a relative error of at most 0.017.
Values may be sent and summed in bfloat16 or wider, within the bound.
No kernel may reach another device: no remote copies, remote signals or barrier semaphores. Data moves between devices by JAX's collectives and lax.ppermute only.
A program may use at most 192 MiB of HBM per device.

v0:
```python
import functools

import jax
import jax.numpy as jnp
from jax import lax
from jax.experimental import pallas as pl
from jax.experimental.pallas import tpu as pltpu
from jax.sharding import PartitionSpec as P

HEAD_DIM = 64
BOTH = ("dp", "tensor")
BIT_Y, BIT_CORE, BIT_X, BIT_Z = 1, 2, 4, 8
PLACES = 32

norm_eps = 1e-12
bf16 = jnp.bfloat16
f32 = jnp.float32


def norm_backward(grad, normed, inverse, gain):
    scaled = grad * gain
    inner = (
        scaled
        - jnp.mean(scaled, axis=-1, keepdims=True)
        - normed * jnp.mean(scaled * normed, axis=-1, keepdims=True)
    )
    return inner * inverse


def dot(left, right):
    return jnp.dot(left, right, preferred_element_type=f32)


def dot_nt(left, right):
    return lax.dot_general(left, right, (((1,), (1,)), ((), ())), preferred_element_type=f32)


def dot_tn(left, right):
    return lax.dot_general(left, right, (((0,), (0,)), ((), ())), preferred_element_type=f32)


def three_parts(value):
    high = value.astype(bf16)
    rest = value - high.astype(f32)
    middle = rest.astype(bf16)
    low = (rest - middle.astype(f32)).astype(bf16)
    return high.astype(f32), middle.astype(f32), low.astype(f32)


def key_bias(length, own, count):
    place = lax.broadcasted_iota(jnp.int32, (count, 128), 0)
    place = (place + own * (count // 2)) & (count - 1)
    return jnp.where(place < length, 0.0, -1000000000.0)


def attend_kernel(info_ref, q_ref, k_ref, v_ref, _c, _l, ctx_ref, lse_ref, *, seq):
    count = q_ref.shape[0]
    lane = lax.broadcasted_iota(jnp.int32, (count, 128), 1)
    bias = key_bias(info_ref[1 + seq], info_ref[0], count)
    query = q_ref[...].astype(f32) * (HEAD_DIM**-0.5)
    keys = k_ref[...].astype(f32)
    values = v_ref[...].astype(f32)
    contexts, sums = [], []
    for head in range(2):
        mine = (lane < 64) if head == 0 else (lane >= 64)
        extra = 64 * (1 - head)
        query_h = jnp.where(mine, query, jnp.where(lane == extra, 1.0, 0.0)).astype(bf16)
        keys_h = jnp.where(mine, keys, jnp.where(lane == extra, bias, 0.0)).astype(bf16)
        values_h = jnp.where(mine, values, 1.0).astype(bf16)
        scores = dot_nt(query_h, keys_h)
        peak = jnp.max(scores, axis=1, keepdims=True)
        exponent = jnp.exp(scores - peak).astype(bf16)
        mixed = dot(exponent, values_h)
        total = pltpu.roll(mixed, 64, 1)
        contexts.append(mixed / total)
        sums.append(peak + jnp.log(mixed))
    low = lane < 64
    ctx_ref[...] = jnp.where(low, contexts[0], contexts[1]).astype(bf16)
    lse_ref[...] = jnp.where(low, sums[1], sums[0])


def attend(info, qkv, seqs, seq, ctx, lse):
    rows, triple = qkv.shape
    count, pairs = rows // seqs, triple // 3 // 128
    block = lambda at: pl.BlockSpec((count, 128), lambda p, info: (seq, p + at * pairs))
    return pl.pallas_call(
        functools.partial(attend_kernel, seq=seq),
        grid_spec=pltpu.PrefetchScalarGridSpec(
            num_scalar_prefetch=1,
            grid=(pairs,),
            in_specs=[block(0), block(1), block(2)] + [pl.BlockSpec(memory_space=pl.ANY)] * 2,
            out_specs=[block(0), block(0)],
        ),
        out_shape=[
            jax.ShapeDtypeStruct((rows, triple // 3), bf16),
            jax.ShapeDtypeStruct((rows, triple // 3), f32),
        ],
        input_output_aliases={4: 0, 5: 1} if seq else {},
        compiler_params=pltpu.CompilerParams(vmem_limit_bytes=14 << 20),
        cost_estimate=pl.CostEstimate(
            flops=9 * 10**9, transcendentals=count * count * pairs * 2, bytes_accessed=count * triple * 4
        ),
        name="attend",
    )(info, qkv, qkv, qkv, ctx, lse)


def attend_back_kernel(
    info_ref, q_ref, k_ref, v_ref, ctx_ref, lse_ref, dctx_ref, earlier_ref, grad_ref, sum_ref, *, seq
):
    count = q_ref.shape[0]
    lane = lax.broadcasted_iota(jnp.int32, (count, 128), 1)
    bias = key_bias(info_ref[1 + seq], info_ref[0], count)
    scale = HEAD_DIM**-0.5
    query = q_ref[...].astype(f32) * scale
    query_low = query.astype(bf16)
    keys_low = k_ref[...]
    keys = keys_low.astype(f32)
    values = v_ref[...].astype(f32)
    grad_low = dctx_ref[...]
    grad = grad_low.astype(f32)
    product = grad * ctx_ref[...].astype(f32)
    lse_parts = three_parts(-lse_ref[...])
    outs = []
    for head in range(2):
        mine = (lane < 64) if head == 0 else (lane >= 64)
        at = lane - 64 * (1 - head)
        ones = jnp.where((at >= 1) & (at <= 3), 1.0, 0.0)

        def spread(parts, first):
            high, middle, low = parts
            value = jnp.where(at == 2, middle, jnp.where(at == 3, low, 0.0))
            return jnp.where(at == 1, high, jnp.where(at == 0, first, value))

        query_h = jnp.where(mine, query, spread(lse_parts, 1.0)).astype(bf16)
        keys_h = jnp.where(mine, keys, jnp.where(at == 0, bias, ones)).astype(bf16)
        inner = -jnp.sum(jnp.where(mine, product, 0.0), axis=1, keepdims=True)
        inner = jnp.broadcast_to(inner, (count, 128))
        grad_h = jnp.where(mine, grad, spread(three_parts(inner), 0.0)).astype(bf16)
        values_h = jnp.where(mine, values, ones).astype(bf16)
        probs = jnp.exp(dot_nt(keys_h, query_h))
        grad_probs = dot_nt(values_h, grad_h)
        grad_scores = (probs * grad_probs).astype(bf16)
        grad_values = dot(probs.astype(bf16), grad_low)
        grad_keys = dot(grad_scores, query_low)
        grad_query = dot_tn(grad_scores, keys_low) * scale
        outs.append((grad_query, grad_keys, grad_values))
    low = lane < 64
    for c, (first, second) in enumerate(zip(outs[0], outs[1])):
        at = pl.multiple_of((c * pl.num_programs(0) + pl.program_id(0)) * 128, 128)
        both = jnp.where(low, first, second).astype(bf16)
        grad_ref[:, pl.ds(at, 128)] = both
        total = jnp.sum(both.astype(f32), axis=0, keepdims=True)
        sum_ref[:, pl.ds(at, 128)] = jnp.broadcast_to(total, (8, 128))


def attend_back(info, qkv, ctx, lse, grad_ctx, seqs, seq, earlier):
    rows, triple = qkv.shape
    count, pairs = rows // seqs, triple // 3 // 128
    block = lambda at: pl.BlockSpec((count, 128), lambda p, info: (seq, p + at * pairs))
    return pl.pallas_call(
        functools.partial(attend_back_kernel, seq=seq),
        grid_spec=pltpu.PrefetchScalarGridSpec(
            num_scalar_prefetch=1,
            grid=(pairs,),
            in_specs=[block(0), block(1), block(2), block(0), block(0), block(0)]
            + [pl.BlockSpec(memory_space=pl.ANY)],
            out_specs=[
                pl.BlockSpec((count, triple), lambda p, info: (seq, 0)),
                pl.BlockSpec((8, triple), lambda p, info: (0, 0)),
            ],
        ),
        out_shape=[
            jax.ShapeDtypeStruct((rows, triple), bf16),
            jax.ShapeDtypeStruct((8, triple), f32),
        ],
        input_output_aliases={7: 0} if seq else {},
        compiler_params=pltpu.CompilerParams(vmem_limit_bytes=24 << 20),
        cost_estimate=pl.CostEstimate(
            flops=16 * 10**9, transcendentals=count * count * pairs * 2, bytes_accessed=count * triple * 5
        ),
        name="attend_back",
    )(info, qkv, qkv, qkv, ctx, lse, grad_ctx, earlier)


def gelu_and_slope(value):
    size = jnp.abs(value)
    near = 1.0 / (1.0 + (0.3275911 * 0.7071067811865476) * size)
    bell = jnp.exp(-0.5 * (value * value))
    poly = 0.5 * 1.061405429
    poly = poly * near + 0.5 * -1.453152027
    poly = poly * near + 0.5 * 1.421413741
    poly = poly * near + 0.5 * -0.284496736
    poly = poly * near + 0.5 * 0.254829592
    tail = poly * near * bell
    phi = jnp.where(value >= 0, 1.0 - tail, tail)
    return value * phi, phi + value * (bell * 0.3989422804014327)


def up_kernel(h_ref, w_ref, b_ref, _g, _s, g_ref, s_ref):
    rows = h_ref.shape[0]
    step = 256
    for at in range(0, rows, step):
        part = pl.ds(at, step)
        before = dot(h_ref[part, :], w_ref[...]) + b_ref[...]
        hidden, slope = gelu_and_slope(before)
        g_ref[part, :] = hidden.astype(bf16)
        s_ref[part, :] = slope.astype(bf16)


def up(first_low, w_in, b_in, part, hidden, slope):
    rows, width = first_low.shape
    units = w_in.shape[1]
    step = 512
    steps = units // step // 2
    column = lambda size: pl.BlockSpec((size, step), lambda i: (0, i + part * steps))
    return pl.pallas_call(
        up_kernel,
        grid=(steps,),
        in_specs=[pl.BlockSpec((rows, width), lambda i: (0, 0)), column(width), column(1)]
        + [pl.BlockSpec(memory_space=pl.ANY)] * 2,
        out_specs=[column(rows)] * 2,
        out_shape=[jax.ShapeDtypeStruct((rows, units), bf16)] * 2,
        input_output_aliases={3: 0, 4: 1} if part else {},
        compiler_params=pltpu.CompilerParams(vmem_limit_bytes=18 << 20),
        cost_estimate=pl.CostEstimate(
            flops=9 * 10**9, transcendentals=rows * units // 2, bytes_accessed=rows * units * 2
        ),
        name="up",
    )(first_low, w_in, b_in, hidden, slope)


def normalize(values):
    centered = values - jnp.mean(values, axis=-1, keepdims=True)
    inverse = lax.rsqrt(jnp.mean(centered * centered, axis=-1, keepdims=True) + norm_eps)
    return centered * inverse, inverse


def add_sums(ref, lines):
    @pl.when(pl.program_id(0) == 0)
    def _():
        ref[...] = jnp.zeros(ref.shape, f32)

    for i, line in enumerate(lines):
        ref[i : i + 1, :] += jnp.sum(line, axis=0, keepdims=True)


def out_kernel(ctx_ref, w_ref, x_ref, v_ref, first_ref, low_ref, normed_ref, inverse_ref):
    values = x_ref[...].astype(f32) + dot_nt(ctx_ref[...], w_ref[...]) + v_ref[1:2, :]
    normed, inverse = normalize(values)
    first = normed * v_ref[0:1, :] + v_ref[2:3, :]
    first_ref[...] = first
    low_ref[...] = first.astype(bf16)
    normed_ref[...] = normed
    inverse_ref[...] = jnp.broadcast_to(inverse, inverse_ref.shape)


def down_kernel(
    g_ref, w_ref, first_ref, kept_ref, got_ref, v_ref, out_ref, grad_ref, low_ref, sum_ref
):
    values = first_ref[...] + dot_nt(g_ref[...], w_ref[...]) + v_ref[1:2, :]
    normed, inverse = normalize(values)
    out_ref[...] = (normed * v_ref[0:1, :] + v_ref[2:3, :]).astype(bf16)
    mine = pl.program_id(0) % 2 == 0
    given = jnp.where(mine, kept_ref[0].astype(f32), got_ref[0].astype(f32))
    grad = norm_backward(given, normed, inverse, v_ref[0:1, :])
    grad_ref[...] = grad
    low_ref[...] = grad.astype(bf16)
    add_sums(sum_ref, (given * normed, given, grad))


def back_kernel(
    u_ref, w_ref, second_ref, normed_ref, inverse_ref, v_ref, grad_ref, low_ref, sum_ref
):
    given = dot_nt(u_ref[...], w_ref[...]) + second_ref[...]
    normed = normed_ref[...]
    grad = norm_backward(given, normed, inverse_ref[:, :1], v_ref[0:1, :])
    grad_ref[...] = grad
    low_ref[...] = grad.astype(bf16)
    add_sums(sum_ref, (given * normed, given, grad))


def by_rows(kernel, name, rows, step, ins, outs):
    def spec(shape, kind):
        if kind == "rows":
            return pl.BlockSpec((step, shape[1]), lambda i: (i, 0))
        if kind == "half":
            return pl.BlockSpec((1, step, shape[2]), lambda i: (i // 2, 0, 0))
        return pl.BlockSpec(shape, lambda i: (0, 0))

    shapes = [jax.ShapeDtypeStruct(shape, kind) for shape, kind, _ in outs]
    return pl.pallas_call(
        kernel,
        grid=(rows // step,),
        in_specs=[spec(value.shape, kind) for value, kind in ins],
        out_specs=[spec(shape, kind) for shape, _, kind in outs],
        out_shape=shapes,
        compiler_params=pltpu.CompilerParams(vmem_limit_bytes=30 << 20),
        cost_estimate=pl.CostEstimate(
            flops=2 * rows * ins[1][0].size,
            transcendentals=0,
            bytes_accessed=0,
        ),
        name=name,
    )(*[value for value, _ in ins])


def swap(value, even, odd):
    pairs = [(i, i ^ (odd if i & BIT_CORE else even)) for i in range(PLACES)]
    return lax.ppermute(value, BOTH, pairs)


def slots(me):
    core = (me >> 1) & 1
    for other in (0, 1):
        along = jnp.where((core ^ other) == 0, BIT_X, BIT_Y)
        across = (BIT_X + BIT_Y) - along
        for part, bits in enumerate((0, along, across, BIT_X + BIT_Y)):
            for k in range(4):
                yield other, part, k, me ^ (other * BIT_CORE) ^ bits ^ (k * BIT_Z)


def window(ref, move, place):
    _, rows, _, columns, _, step, start, wide = move
    row = pl.multiple_of((place >> 1 if wide else place) * step, 16)
    if not wide:
        return ref.at[pl.ds(row, rows), :]
    column = pl.multiple_of(start + (place & 1) * columns, 128)
    return ref.at[pl.ds(row, rows), pl.ds(column, columns)]


def place_kernel(me_ref, *refs, moves, outs):
    ins, wholes, sems = refs[:8], refs[8 : 8 + outs], refs[8 + outs]
    for other, part, k, place in slots(me_ref[0]):
        for move in moves:
            row, rows, column, columns, to = move[:5]
            pltpu.make_async_copy(
                ins[4 * other + part].at[k, pl.ds(row, rows), pl.ds(column, columns)],
                window(wholes[to], move, place),
                sems.at[to],
            ).start()
    for to in range(outs):
        pltpu.make_async_copy(wholes[to], wholes[to], sems.at[to]).wait()


def spread_kernel(me_ref, *refs, moves, ins):
    wholes, halves, sems = refs[:ins], refs[ins : ins + 2], refs[ins + 2]
    for other, part, k, place in slots(me_ref[0]):
        for move in moves:
            row, rows, column, columns, to = move[:5]
            pltpu.make_async_copy(
                window(wholes[to], move, place),
                halves[other].at[part, k, pl.ds(row, rows), pl.ds(column, columns)],
                sems.at[other],
            ).start()
    for other in (0, 1):
        pltpu.make_async_copy(halves[other], halves[other], sems.at[other]).wait()


anywhere = pl.BlockSpec(memory_space=pltpu.HBM)
on_core = pl.BlockSpec(memory_space=pltpu.VMEM)


def place(me, parts, moves, shapes):
    return pl.pallas_call(
        functools.partial(place_kernel, moves=moves, outs=len(shapes)),
        in_specs=[pl.BlockSpec(memory_space=pltpu.SMEM)] + [anywhere] * 8,
        out_specs=[on_core] * len(shapes),
        out_shape=[jax.ShapeDtypeStruct(shape, bf16) for shape in shapes],
        compiler_params=pltpu.CompilerParams(vmem_limit_bytes=8 << 20),
        cost_estimate=pl.CostEstimate(
            flops=4 * 10**9, transcendentals=0, bytes_accessed=0
        ),
        scratch_shapes=[pltpu.SemaphoreType.DMA((len(shapes),))],
        name="place",
    )(me, *parts)


def spread(me, wholes, moves, rows, columns):
    return pl.pallas_call(
        functools.partial(spread_kernel, moves=moves, ins=len(wholes)),
        in_specs=[pl.BlockSpec(memory_space=pltpu.SMEM)] + [anywhere] * len(wholes),
        out_specs=[on_core] * 2,
        out_shape=[jax.ShapeDtypeStruct((4, 4, rows, columns), bf16)] * 2,
        compiler_params=pltpu.CompilerParams(vmem_limit_bytes=8 << 20),
        cost_estimate=pl.CostEstimate(
            flops=2 * 10**9, transcendentals=0, bytes_accessed=0
        ),
        scratch_shapes=[pltpu.SemaphoreType.DMA((2,))],
        name="spread",
    )(me, *wholes)


def lines_kernel(v_ref, lines_ref, b_ref, *, count, wide):
    places = v_ref.shape[0] // 16
    for place in range(places):
        line = v_ref[pl.ds(place * 16, 16), :].astype(f32)[0:1]
        to = (place % 2) * (places // 2) + place // 2
        starts = [0, count] + [2 * count + wide + i * count for i in range(6)]
        for i, start in enumerate(starts):
            lines_ref[i : i + 1, to * count : (to + 1) * count] = line[:, start : start + count]
        b_ref[:, to * wide : (to + 1) * wide] = line[:, 2 * count : 2 * count + wide]


def unpack_lines(vector_rows, count, wide):
    places = vector_rows.shape[0] // 16
    return pl.pallas_call(
        functools.partial(lines_kernel, count=count, wide=wide),
        out_shape=[
            jax.ShapeDtypeStruct((8, places * count), f32),
            jax.ShapeDtypeStruct((1, places * wide), f32),
        ],
        name="lines",
    )(vector_rows)


def shares_kernel(sums_ref, b_ref, one_ref, two_ref, out_ref, held_ref, *, count, wide, width):
    held_ref[...] = jnp.zeros(held_ref.shape, f32)
    places = held_ref.shape[0] // 16
    for place in range(places):
        at = slice(place * 16, place * 16 + 1)
        to = (place % 2) * (places // 2) + place // 2
        own = slice(to * count, (to + 1) * count)
        last = slice(2 * width + to * count, 2 * width + (to + 1) * count)
        held_ref[at, :count] = sums_ref[0:1, own]
        held_ref[at, count : 2 * count] = sums_ref[0:1, last]
        held_ref[at, 2 * count : 2 * count + wide] = b_ref[:, to * wide : (to + 1) * wide]
        lines = ((one_ref, 0), (two_ref, 0), (one_ref, 2), (one_ref, 1), (two_ref, 2), (two_ref, 1))
        for i, (ref, line) in enumerate(lines):
            start = 2 * count + wide + i * count
            held_ref[at, start : start + count] = ref[line : line + 1, own]
    out_ref[...] = held_ref[...].astype(bf16)


def pack_shares(sums, b_sum, one, two, places, columns, count, wide):
    width = one.shape[1]
    return pl.pallas_call(
        functools.partial(shares_kernel, count=count, wide=wide, width=width),
        out_shape=jax.ShapeDtypeStruct((places * 16, columns), bf16),
        scratch_shapes=[pltpu.VMEM((places * 16, columns), f32)],
        name="shares",
    )(sums, b_sum, one, two)


def move_list(row, blocks, vectors=None):
    moves, at = [], -row
    for to, column, columns, start in blocks:
        at = at if column else at + row
        moves.append((at, row, column, columns, to, row, start, True))
    if vectors:
        moves.append((at + row, 16, 0, blocks[0][2], vectors, 16, 0, False))
    return tuple(moves)


def sync(*values):
    return lax.optimization_barrier(values)


def along_z(shard, direct):
    return [shard] + [swap(shard, BIT_Z * k, BIT_Z * k) for k in (1, 2, 3) if direct]


def far_z(shard, direct):
    return [shard] + [swap(shard, 2 * BIT_Z, 2 * BIT_Z) for _ in (0,) if direct]


def near_z(held, direct):
    if not direct:
        return held
    pair = jnp.stack(held)
    got = swap(pair, BIT_Z, BIT_Z)
    return [pair[0], got[0], pair[1], got[1]]


class Gather:
    def __init__(self, me, group, moves, shapes, direct, early=False):
        self.me, self.moves, self.shapes, self.direct = me, moves, shapes, direct
        self.early = early
        self.held, self.stage = group, 0

    def step(self):
        self.stage += 1
        held = self.held
        if not self.direct:
            return
        if self.stage == 1:
            group = jnp.stack(held)
            self.held = [group, swap(group, BIT_X, BIT_Y), swap(group, BIT_Y, BIT_X)]
            if self.early:
                self.held.append(swap(group, BIT_CORE, BIT_CORE))
        elif self.stage == 2:
            corner = swap(held[1], BIT_Y, BIT_X)
            got = held[3:] + [swap(part, BIT_CORE, BIT_CORE) for part in held[len(held) - 3 : 3]]
            self.held = held[:3] + [corner] + got
        else:
            self.held = held + [swap(held[3], BIT_CORE, BIT_CORE)]

    def whole(self):
        if self.direct:
            return place(self.me, self.held, self.moves, self.shapes)
        everything = lax.all_gather(self.held[0], BOTH, axis=0)
        places = everything.shape[0]
        wholes = []
        for to, shape in enumerate(self.shapes):
            pieces = []
            for row, rows, column, columns, at, _, _, wide in self.moves:
                if at != to:
                    continue
                piece = everything[:, row : row + rows, column : column + columns]
                if wide:
                    piece = piece.reshape(places // 2, 2, rows, columns).transpose(0, 2, 1, 3)
                    pieces.append(piece.reshape(places // 2 * rows, 2 * columns))
                else:
                    pieces.append(piece.reshape(shape))
            wholes.append(jnp.concatenate(pieces, axis=1))
        return wholes


def add_low(*parts):
    return sum(part.astype(f32) for part in parts).astype(bf16)


class Reduce:
    def __init__(self, me, wholes, moves, rows, columns, direct, folded=False):
        self.direct, self.stage, self.folded = direct, 0, folded
        if direct:
            self.held = spread(me, wholes, moves, rows, columns)
            return
        pieces = []
        for _, count, _, wide_columns, to, step, start, wide in moves:
            whole = wholes[to]
            if wide:
                whole = whole[:, start : start + 2 * wide_columns]
                whole = whole.reshape(-1, count, 2, wide_columns).transpose(0, 2, 1, 3)
            pieces.append(whole.reshape(-1, count, wide_columns))
        self.held = [jnp.concatenate(pieces, axis=1)]

    def step(self):
        self.stage += 1
        held = self.held
        if not self.direct:
            return
        if self.stage == 1:
            self.held = [held[0], swap(held[1], BIT_CORE, BIT_CORE)]
        elif self.stage == 2:
            total = [add_low(held[0][at], held[1][at]) for at in range(4)]
            self.held = total[:2] + [swap(total[at], BIT_Y, BIT_X) for at in (2, 3)]
        elif self.stage == 3:
            group, near, far, corner = held
            self.held = [group, far, swap(add_low(near, corner), BIT_X, BIT_Y)]
        elif self.folded and self.stage == 4:
            group = add_low(*held)
            self.held = [group[:2], swap(group[2:], 2 * BIT_Z, 2 * BIT_Z)]
        elif self.folded:
            group = add_low(*held)
            self.held = [group[0], swap(group[1], BIT_Z, BIT_Z)]
        else:
            group = add_low(*held)
            self.held = [group[0]] + [swap(group[k], BIT_Z * k, BIT_Z * k) for k in (1, 2, 3)]

    def shard(self):
        if not self.direct:
            return lax.psum_scatter(self.held[0], BOTH, scatter_dimension=0, tiled=True)[
                0
            ].astype(f32)
        return sum(part.astype(f32) for part in self.held)


def shards(
    tokens, lengths, w_qkv, qkv_bias, w_out, w_in, b_in, w_down, norm_gains, row_biases, cotangent, direct
):
    half_len, seq_count, width = tokens.shape
    own = lax.axis_index("tensor")
    me = (lax.axis_index("dp") * 2 + own).astype(jnp.int32).reshape(1)
    seqs = seq_count // 2
    row = w_qkv.shape[1]
    local_width, local_units = w_qkv.shape[2], w_in.shape[1]
    count = qkv_bias.shape[1]
    units = 2 * local_units
    places = width // row * 2
    total_rows = seqs * 2 * half_len

    def trade(value):
        return lax.ppermute(value, "tensor", [(0, 1), (1, 0)])

    def split_rows(value):
        by_seq = jnp.swapaxes(value, 0, 1)
        kept = lax.dynamic_slice_in_dim(by_seq, own * seqs, seqs, 0)
        return kept, lax.dynamic_slice_in_dim(by_seq, (1 - own) * seqs, seqs, 0)

    def to_rows(value):
        kept, sent = split_rows(value)
        return [kept, trade(sent)]

    def as_rows(halves):
        return jnp.stack(halves, axis=1).reshape(total_rows, width)

    def from_rows(kept, got, kind):
        first = jnp.where(own == 0, kept, got)
        second = jnp.where(own == 0, got, kept)
        return jnp.swapaxes(jnp.concatenate([first, second], axis=0), 0, 1).astype(kind)

    def pack(pieces, kind):
        flat = jnp.concatenate([piece.reshape(piece.shape[0], -1) for piece in pieces], axis=1)
        flat = jnp.pad(flat, ((0, 0), (0, local_width - flat.shape[1])))
        return jnp.pad(flat[:, None, :], ((0, 0), (0, 15), (0, 0))).astype(kind)

    vectors = pack(
        [qkv_bias[None], b_in[None], norm_gains[None], row_biases[None]], bf16
    ).reshape(16, local_width)
    attn_shard = jnp.concatenate([w_qkv.reshape(3 * row, local_width), vectors], axis=0)
    qkv_blocks = [(0, 0, local_width, c * width) for c in range(3)]
    qkv_moves = move_list(row, qkv_blocks, 1)
    upper_moves = move_list(row, [(0, 0, local_units, 0), (1, local_units, local_width, 0)])
    mlp_moves = move_list(row, [(0, 0, local_units, 0)])
    out_moves = move_list(row, [(0, 0, local_width, 0)])
    attn_shapes = [(width, 3 * width), (places * 16, local_width)]

    attn_shard, tokens = sync(attn_shard, tokens)
    attn = Gather(me, along_z(attn_shard, direct), qkv_moves, attn_shapes, direct)
    kept, sent = split_rows(tokens)
    got = [trade(sent[:1])]
    over, under = jnp.concatenate([w_in, w_out.T], axis=1), w_down.T
    attn.held, over, under, kept, got, sent = sync(attn.held, over, under, kept, got, sent)
    attn.step()
    got.append(trade(sent[1:]))
    over = far_z(over, direct)
    under = far_z(under, direct)
    attn.held, over, under, kept, got = sync(attn.held, over, under, kept, got)
    attn.step()
    over = near_z(over, direct)
    rows = as_rows([kept, jnp.concatenate(got, axis=0)])
    attn.held, over, under, rows = sync(attn.held, over, under, rows)
    upper_shapes = [(width, units), (width, width)]
    upper = Gather(me, over, upper_moves, upper_shapes, direct, early=True)
    attn.step()
    under = near_z(under, direct)
    upper.step()
    lower = Gather(me, under, mlp_moves, [(width, units)], direct)
    wq, vector_rows = attn.whole()
    wide = b_in.shape[0]
    if direct:
        lines, b_in_all = unpack_lines(vector_rows, count, wide)
        bias_pair, gains, shifts = lines[:2], lines[2:4], lines[4:]
    else:
        flat = vector_rows.reshape(places // 2, 2, 16, local_width)[:, :, 0]
        flat = jnp.swapaxes(flat, 0, 1).reshape(places, local_width).astype(f32)

        def vector(at, lines, size):
            piece = flat[:, at : at + lines * size].reshape(places, lines, size)
            return jnp.swapaxes(piece, 0, 1).reshape(lines, places * size)

        bias_pair, b_in_all = vector(0, 2, count), vector(2 * count, 1, wide)
        gains, shifts = vector(2 * count + wide, 2, count), vector(4 * count + wide, 4, count)

    mine_lengths = lax.dynamic_slice_in_dim(lengths, own * seqs, seqs, 0)
    info = jnp.concatenate([own.reshape(1).astype(jnp.int32), mine_lengths])

    upper.held, wq, bias_pair = sync(upper.held, wq, bias_pair)
    upper.step()
    qkv_shift = jnp.concatenate([bias_pair[0], jnp.zeros((width,), f32), bias_pair[1]])
    qkv = (dot(rows, wq) + qkv_shift).astype(bf16)
    lower.held, qkv = sync(lower.held, qkv)
    lower.step()
    ctx, lse = attend(info, qkv, seqs, 0, qkv, qkv)
    for seq in range(1, seqs):
        upper.held, ctx, lse = sync(upper.held, ctx, lse)
        if seq == 1:
            upper.step()
        ctx, lse = attend(info, qkv, seqs, seq, ctx, lse)
    upper.held, lower.held, ctx, cotangent = sync(upper.held, lower.held, ctx, cotangent)
    lower.step()
    grad_halves = to_rows(cotangent)
    wi, wo = upper.whole()
    one_lines = jnp.stack([gains[0], shifts[0], shifts[1]])
    two_lines = jnp.stack([gains[1], shifts[2], shifts[3]])
    wide_rows = (total_rows, width)
    first, first_low, normed_one, inverse_one = by_rows(
        out_kernel,
        "attention_out",
        total_rows,
        half_len,
        [(ctx, "rows"), (wo, "whole"), (rows, "rows"), (one_lines, "whole")],
        [
            (wide_rows, f32, "rows"),
            (wide_rows, bf16, "rows"),
            (wide_rows, f32, "rows"),
            ((total_rows, 128), f32, "rows"),
        ],
    )
    hidden, slope = up(first_low, wi, b_in_all, 0, first_low, first_low)
    lower.held, hidden, slope = sync(lower.held, hidden, slope)
    lower.step()
    hidden, slope = up(first_low, wi, b_in_all, 1, hidden, slope)
    lower.held, hidden, grad_halves = sync(lower.held, hidden, grad_halves)
    (wd,) = lower.whole()
    output, grad_second, mixed_grad, two_sums = by_rows(
        down_kernel,
        "down",
        total_rows,
        half_len,
        [
            (hidden, "rows"),
            (wd, "whole"),
            (first, "rows"),
            (grad_halves[0], "half"),
            (grad_halves[1], "half"),
            (two_lines, "whole"),
        ],
        [
            (wide_rows, bf16, "rows"),
            (wide_rows, f32, "rows"),
            (wide_rows, bf16, "rows"),
            ((8, width), f32, "whole"),
        ],
    )
    by_half = output.reshape(seqs, 2, half_len, width)
    early, late, mixed_grad, hidden = sync(by_half[:1, 1], by_half[1:, 1], mixed_grad, hidden)
    early = trade(early)
    grad_wd = dot_tn(mixed_grad, hidden).astype(bf16)
    down = Reduce(me, [grad_wd], mlp_moves, row, local_units, direct, folded=True)
    down.held, mixed_grad, early, late = sync(down.held, mixed_grad, early, late)
    late = trade(late)
    down.step()
    grad_before = (dot(mixed_grad, wd) * slope.astype(f32)).astype(bf16)
    down.held, grad_before, late = sync(down.held, grad_before, late)
    down.step()
    grad_in_bias = jnp.sum(grad_before, axis=0, dtype=f32)
    grad_wi = dot_tn(first_low, grad_before).astype(bf16)
    into = Reduce(me, [grad_wi], mlp_moves, row, local_units, direct, folded=True)
    into.held, grad_before = sync(into.held, grad_before)
    into.step()
    grad_resid, attn_grad, one_sums = by_rows(
        back_kernel,
        "up_back",
        total_rows,
        half_len,
        [
            (grad_before, "rows"),
            (wi, "whole"),
            (grad_second, "rows"),
            (normed_one, "rows"),
            (inverse_one, "rows"),
            (one_lines, "whole"),
        ],
        [(wide_rows, f32, "rows"), (wide_rows, bf16, "rows"), ((8, width), f32, "whole")],
    )
    grad_wo = dot_tn(attn_grad, ctx).astype(bf16)
    grad_ctx = dot(attn_grad, wo).astype(bf16)
    down.held, into.held, grad_wo, grad_ctx = sync(down.held, into.held, grad_wo, grad_ctx)
    down.step()
    into.step()
    outer = Reduce(me, [grad_wo], out_moves, row, local_width, direct, folded=True)
    outer.step()
    count_rows = total_rows // seqs
    grad_triple, sums = attend_back(info, qkv, ctx, lse, grad_ctx, seqs, 0, qkv)
    token_halves = []

    def token_grads(seq):
        mine = slice(seq * count_rows, (seq + 1) * count_rows)
        value = dot_nt(grad_triple[mine], wq) + grad_resid[mine]
        return value[:half_len], value[half_len:].astype(bf16)

    for seq in range(1, seqs):
        first_held = into.held[:3]
        down.held, first_held, outer.held, token_halves, grad_triple = sync(
            down.held, first_held, outer.held, token_halves, grad_triple
        )
        into.held = first_held + into.held[3:]
        if seq == 1:
            down.step()
            outer.step()
        kept, sent = token_grads(seq - 1)
        grad_triple, kept, sent = sync(grad_triple, kept, sent)
        token_halves.append([kept, trade(sent)])
        grad_triple, more = attend_back(info, qkv, ctx, lse, grad_ctx, seqs, seq, grad_triple)
        sums = sums + more
    down.held, into.held, outer.held, token_halves, grad_triple = sync(
        down.held, into.held, outer.held, token_halves, grad_triple
    )
    into.step()
    grad_wq = dot_tn(rows, grad_triple).astype(bf16)

    if direct:
        grad_vectors = pack_shares(
            sums, grad_in_bias[None], one_sums, two_sums, places, local_width, count, wide
        )
    else:

        def shares(value, lines):
            size = value.size // lines // places
            piece = value.reshape(lines, 2, places // 2, size)
            return piece.transpose(2, 1, 0, 3).reshape(places, lines * size)

        grad_pair = jnp.stack([sums[0, :width], sums[0, 2 * width :]])
        one, two = one_sums, two_sums
        grad_lines = [one[0], two[0], one[2], one[1], two[2], two[1]]
        grad_vectors = pack(
            [shares(grad_pair, 2), shares(grad_in_bias, 1), shares(jnp.stack(grad_lines), 6)], bf16
        ).reshape(places * 16, local_width)
    triple = Reduce(
        me, [grad_wq, grad_vectors], qkv_moves, 3 * row + 16, local_width, direct
    )
    triple.held, grad_triple = sync(triple.held, grad_triple)
    triple.step()
    kept, sent = token_grads(seqs - 1)
    triple.held, into.held, kept, sent = sync(triple.held, into.held, kept, sent)
    triple.step()
    into.step()
    down.step()
    outer.step()
    triple.held, down.held, into.held, outer.held, early, late, by_half = sync(
        triple.held, down.held, into.held, outer.held, early, late, by_half
    )
    triple.step()
    into.step()
    outer.step()
    out = from_rows(by_half[:, 0], jnp.concatenate([early, late]), bf16)
    triple.held, into.held, outer.held, sent, out = sync(
        triple.held, into.held, outer.held, sent, out
    )
    triple.step()
    outer.step()
    token_halves.append([kept, trade(sent)])
    d_tokens = from_rows(
        jnp.stack([kept for kept, _ in token_halves]),
        jnp.stack([got for _, got in token_halves]).astype(f32),
        f32,
    )
    grad_down = down.shard().T
    grad_in = into.shard()
    grad_out = outer.shard().T
    attn_piece = triple.shard()
    grad_qkv = attn_piece[: 3 * row].reshape(3, row, local_width)
    line = attn_piece[3 * row]

    def cut(at, lines, size):
        return line[at : at + lines * size].reshape(lines, size)

    return (
        out,
        d_tokens,
        grad_qkv,
        cut(0, 2, count),
        grad_out,
        grad_in,
        cut(2 * count, 1, wide)[0],
        grad_down,
        cut(2 * count + wide, 2, count),
        cut(4 * count + wide, 4, count),
    )


def solution(mesh):
    placed = (
        P("tensor", "dp", None),
        P("dp"),
        P(None, "dp", "tensor"),
        P(None, ("tensor", "dp")),
        P("tensor", "dp"),
        P("dp", "tensor"),
        P(("tensor", "dp")),
        P("tensor", "dp"),
        P(None, ("tensor", "dp")),
        P(None, ("tensor", "dp")),
        P("tensor", "dp", None),
    )
    direct = mesh.shape["tensor"] == 2 and mesh.shape["dp"] * 2 == PLACES
    return jax.shard_map(
        functools.partial(shards, direct=direct),
        mesh=mesh,
        in_specs=placed,
        out_specs=(
            P("tensor", "dp", None),
            P("tensor", "dp", None),
            P(None, "dp", "tensor"),
            P(None, ("tensor", "dp")),
            P("tensor", "dp"),
            P("dp", "tensor"),
            P(("tensor", "dp")),
            P("tensor", "dp"),
            P(None, ("tensor", "dp")),
            P(None, ("tensor", "dp")),
        ),
        check_vma=False,
    )
```

profile of v0, /device:TPU:0, one launch (start us, length us, event | category | flops | bytes accessed | tf_op | source)
XLA Modules:
  0.0 323.0 jit_solution(7262040210731547643)
XLA Ops:
  6.4 3.0 collective-permute-start.3
  11.0 2.6 collective-permute-start.1
  13.8 1.8 collective-permute-done
  15.6 7.4 %collective-permute-done.1 = bf16[160,384]{1,0:T(8,128)(2,1)S(1)} collective-permute-done((bf16[160,384]{1,0:T(8,128)(2,1)S(1)}, bf16[160,384]{1,0:T(8,128)(2,1)S(1)}, u32[]{:S(2)}, u32[]{:S(2)}) %collective-permute-start.1) | collective-permute-done | bytes 122912 | tf_op jit(solution)/shard_map/ppermute | solution.py:309
  26.8 2.9 collective-permute-start.6
  29.7 12.6 %collective-permute-done.7 = bf16[48,1536]{1,0:T(8,128)(2,1)S(1)} collective-permute-done((bf16[48,1536]{1,0:T(8,128)(2,1)S(1)}, bf16[48,1536]{1,0:T(8,128)(2,1)S(1)}, u32[]{:S(2)}, u32[]{:S(2)}) %collective-permute-start.7) | collective-permute-done | bytes 147488 | tf_op jit(solution)/shard_map/ppermute | solution.py:309
  42.4 2.7 collective-permute-start.13
  47.3 4.5 %collective-permute-done.13 = bf16[2,48,1920]{2,1,0:T(8,128)(2,1)S(1)} collective-permute-done((bf16[2,48,1920]{2,1,0:T(8,128)(2,1)S(1)}, bf16[2,48,1920]{2,1,0:T(8,128)(2,1)S(1)}, u32[]{:S(2)}, u32[]{:S(2)}) %collective-permute-start.13) | collective-permute-done | bytes 368672 | tf_op jit(solution)/shard_map/ppermute | solution.py:309
  58.2 5.6 %collective-permute-done.21 = bf16[2,48,1536]{2,1,0:T(8,128)(2,1)} collective-permute-done((bf16[2,48,1536]{2,1,0:T(8,128)(2,1)}, bf16[2,48,1536]{2,1,0:T(8,128)(2,1)}, u32[]{:S(2)}, u32[]{:S(2)}) %collective-permute-start.21) | collective-permute-done | bytes 294944 | tf_op jit(solution)/shard_map/ppermute | solution.py:309
  66.6 2.0 place.3
  69.4 1.9 copy-done.32
  71.3 1.8 lines.1
  76.6 6.1 %add_convert_fusion.q_ref.k_ref.v_ref._c._l.earlier_ref = bf16[1024,2304]{1,0:T(8,128)(2,1)S(1)} fusion(bf16[1024,768]{1,0:T(8,128)(2,1)S(1)} %bitcast.144, bf16[768,2304]{1,0:T(8,128)(2,1)} %copy-done.32, f32[2304]{0:T(1024)S(1)} %pad_maximum_fusion.10), kind=kOutput, calls=%fused_computation.2 | convolution fusion | flops 3628597248 | bytes 9839616 | tf_op jit(solution)/shard_map/dot_general | solution.py:31
  85.3 8.2 %attend.2 = (bf16[1024,768]{1,0:T(8,128)(2,1)S(1)}, f32[1024,768]{1,0:T(8,128)S(1)}) custom-call(s32[3]{0:T(128)S(1)} %pad_add_fusion.info_ref, bf16[1024,2304]{1,0:T(8,128)(2,1)S(1)} %add_convert_fusion.q_ref.k_ref.v_ref._c._l.earlier_ref, bf16[1024,2304]{1,0:T(8,128)(2,1)S(1)} %add_convert_fusion.q_ref.k_ref.v_ref._c._l.earlier_ref, ...), custom_call_target="tpu_custom_call" | custom-call | flops 8999999488 | bytes 4718592 | tf_op jit(solution)/shard_map/attend/pallas_call | solution.py:86
  94.1 8.2 %attend.3 = (bf16[1024,768]{1,0:T(8,128)(2,1)S(1)}, f32[1024,768]{1,0:T(8,128)S(1)}) custom-call(s32[3]{0:T(128)S(1)} %pad_add_fusion.info_ref, bf16[1024,2304]{1,0:T(8,128)(2,1)S(1)} %add_convert_fusion.q_ref.k_ref.v_ref._c._l.earlier_ref, ...), custom_call_target="tpu_custom_call", output_to_operand_aliasing={{0}: (4, {}), {1}: (5, {})} | custom-call | flops 8999999488 | bytes 4718592 | tf_op jit(solution)/shard_map/attend/pallas_call | solution.py:86
  107.1 1.8 place.4
  109.0 3.3 %attention_out.1 = (f32[1024,768]{1,0:T(8,128)S(1)}, bf16[1024,768]{1,0:T(8,128)(2,1)S(1)}, f32[1024,768]{1,0:T(8,128)S(1)}, f32[1024,128]{1,0:T(8,128)S(1)}) custom-call(bf16[1024,768]{1,0:T(8,128)(2,1)S(1)} %get-tuple-element.281.ctx_ref, bf16[768,768]{1,0:T(8,128)(2,1)S(1)} %get-tuple-element.290.w_ref, bf16[1024,768]{1,0:T(8,128)(2,1)S(1)} %bitcast.145, ...), custom_call_target="tpu_custom_call" | custom-call | flops 1207959552 | tf_op jit(solution)/shard_map/attention_out/pallas_call | solution.py:291
  113.3 8.0 %up.2 = (bf16[1024,3072]{1,0:T(8,128)(2,1)S(1)}, bf16[1024,3072]{1,0:T(8,128)(2,1)S(1)}) custom-call(bf16[1024,768]{1,0:T(8,128)(2,1)S(1)} %get-tuple-element.291.h_ref._g._s, bf16[768,3072]{1,0:T(8,128)(2,1)S(1)} %get-tuple-element.292.w_ref, f32[1,3072]{1,0:T(1,128)S(1)} %copy-done.14, bf16[1024,768]{1,0:T(8,128)(2,1)S(1)} %get-tuple-element.291.h_ref._g._s, ...), custom_call_target="tpu_custom_call" | custom-call | flops 8999999488 | bytes 6291456 | tf_op jit(solution)/shard_map/up/pallas_call | solution.py:216
  121.6 8.1 %up.3 = (bf16[1024,3072]{1,0:T(8,128)(2,1)S(1)}, bf16[1024,3072]{1,0:T(8,128)(2,1)S(1)}) custom-call(bf16[1024,768]{1,0:T(8,128)(2,1)S(1)} %get-tuple-element.291.h_ref._g._s, bf16[768,3072]{1,0:T(8,128)(2,1)S(1)} %get-tuple-element.292.w_ref, f32[1,3072]{1,0:T(1,128)S(1)} %copy-done.14, ...), custom_call_target="tpu_custom_call", output_to_operand_aliasing={{0}: (3, {}), {1}: (4, {})} | custom-call | flops 8999999488 | bytes 6291456 | tf_op jit(solution)/shard_map/up/pallas_call | solution.py:216
  132.5 1.8 copy-done.35
  134.3 2.8 copy-done.30
  137.1 8.6 %down.1 = (bf16[1024,768]{1,0:T(8,128)(2,1)S(1)}, f32[1024,768]{1,0:T(8,128)S(1)}, bf16[1024,768]{1,0:T(8,128)(2,1)S(1)}, f32[8,768]{1,0:T(8,128)S(1)}) custom-call(bf16[1024,3072]{1,0:T(8,128)(2,1)S(1)} %copy-done.30, bf16[768,3072]{1,0:T(8,128)(2,1)S(1)} %place.5.w_ref, f32[1024,768]{1,0:T(8,128)S(1)} %get-tuple-element.316.first_ref, ...), custom_call_target="tpu_custom_call" | custom-call | flops 4831838208 | tf_op jit(solution)/shard_map/down/pallas_call | solution.py:291
  146.2 5.4 %convolution_convert_fusion.1.refs_0_ = bf16[768,3072]{1,0:T(8,128)(2,1)S(1)} fusion(bf16[1024,768]{1,0:T(8,128)(2,1)S(1)} %get-tuple-element.329, bf16[1024,3072]{1,0:T(8,128)(2,1)S(1)} %copy-done.30), kind=kOutput, calls=%fused_computation.4 | convolution fusion | flops 4834197504 | bytes 12582912 | tf_op jit(solution)/shard_map/dot_general | solution.py:39
  152.8 4.3 %collective-permute-done.31 = bf16[1,256,768]{2,1,0:T(8,128)(2,1)S(1)} collective-permute-done((bf16[1,256,768]{2,1,0:T(8,128)(2,1)S(1)}, bf16[1,256,768]{2,1,0:T(8,128)(2,1)S(1)}, u32[]{:S(2)}, u32[]{:S(2)}) %collective-permute-start.31) | collective-permute-done | bytes 393248 | tf_op jit(solution)/shard_map/ppermute | solution.py:583
  157.9 7.3 %multiply_convert_fusion.u_ref = bf16[1024,3072]{1,0:T(8,128)(2,1)S(1)} fusion(bf16[1024,3072]{1,0:T(8,128)(2,1)} %copy-done.35, bf16[1024,768]{1,0:T(8,128)(2,1)S(1)} %get-tuple-element.329, bf16[768,3072]{1,0:T(8,128)(2,1)S(1)} %place.5.w_ref), kind=kOutput, calls=%fused_computation.1 | convolution fusion | flops 4841275392 | bytes 18874368 | tf_op jit(solution)/shard_map/dot_general | solution.py:31
  165.2 3.5 %collective-permute-done.33 = bf16[1,256,768]{2,1,0:T(8,128)(2,1)S(1)} collective-permute-done((bf16[1,256,768]{2,1,0:T(8,128)(2,1)S(1)}, bf16[1,256,768]{2,1,0:T(8,128)(2,1)S(1)}, u32[]{:S(2)}, u32[]{:S(2)}) %collective-permute-start.33) | collective-permute-done | bytes 393248 | tf_op jit(solution)/shard_map/ppermute | solution.py:583
  168.7 5.4 %convolution_convert_fusion.refs_0_ = bf16[768,3072]{1,0:T(8,128)(2,1)S(1)} fusion(bf16[1024,768]{1,0:T(8,128)(2,1)S(1)} %copy-done.24, bf16[1024,3072]{1,0:T(8,128)(2,1)S(1)} %multiply_convert_fusion.u_ref), kind=kOutput, calls=%fused_computation.3 | convolution fusion | flops 4834197504 | bytes 12582912 | tf_op jit(solution)/shard_map/dot_general | solution.py:39
  175.8 3.4 %fusion.11 = (bf16[4,48,1536]{2,1,0:T(8,128)(2,1)}, bf16[4,48,1536]{2,1,0:T(8,128)(2,1)}, bf16[4,48,1536]{2,1,0:T(8,128)(2,1)S(1)}, bf16[4,48,1536]{2,1,0:T(8,128)(2,1)}) fusion(bf16[4,4,48,1536]{3,2,1,0:T(8,128)(2,1)} %collective-permute-done.32, bf16[4,4,48,1536]{3,2,1,0:T(8,128)(2,1)S(1)} %get-tuple-element.332), kind=kLoop, calls=%fused_computation.52 | loop fusion | flops 4718592 | bytes 7077888 | tf_op jit(solution)/shard_map/convert_element_type | solution.py:519
  181.2 2.3 copy-done.16
  183.6 1.9 copy-done.20
  185.5 7.3 %up_back.1 = (f32[1024,768]{1,0:T(8,128)S(1)}, bf16[1024,768]{1,0:T(8,128)(2,1)S(1)}, f32[8,768]{1,0:T(8,128)S(1)}) custom-call(bf16[1024,3072]{1,0:T(8,128)(2,1)S(1)} %multiply_convert_fusion.u_ref, bf16[768,3072]{1,0:T(8,128)(2,1)S(1)} %copy-done.16, f32[1024,768]{1,0:T(8,128)S(1)} %copy-done.22, f32[1024,768]{1,0:T(8,128)S(1)} %copy-done.20, ...), custom_call_target="tpu_custom_call" | custom-call | flops 4831838208 | tf_op jit(solution)/shard_map/up_back/pallas_call | solution.py:291
  197.9 3.4 %fusion.15 = (bf16[4,48,1536]{2,1,0:T(8,128)(2,1)}, bf16[4,48,1536]{2,1,0:T(8,128)(2,1)S(1)}, bf16[4,48,1536]{2,1,0:T(8,128)(2,1)}, bf16[4,48,1536]{2,1,0:T(8,128)(2,1)}) fusion(bf16[4,4,48,1536]{3,2,1,0:T(8,128)(2,1)} %collective-permute-done.36, bf16[4,4,48,1536]{3,2,1,0:T(8,128)(2,1)S(1)} %get-tuple-element.348), kind=kLoop, calls=%fused_computation.56 | loop fusion | flops 4718592 | bytes 7077888 | tf_op jit(solution)/shard_map/convert_element_type | solution.py:519
  205.8 12.5 %attend_back.2 = (bf16[1024,2304]{1,0:T(8,128)(2,1)S(1)}, f32[8,2304]{1,0:T(8,128)S(1)}) custom-call(s32[3]{0:T(128)S(1)} %pad_add_fusion.info_ref, bf16[1024,2304]{1,0:T(8,128)(2,1)S(1)} %bitcast.152, bf16[1024,2304]{1,0:T(8,128)(2,1)S(1)} %bitcast.152, bf16[1024,2304]{1,0:T(8,128)(2,1)S(1)} %bitcast.152, bf16[1024,768]{1,0:T(8,128)(2,1)S(1)} %copy-done.26, ...), custom_call_target="tpu_custom_call" | custom-call | flops 16000000000 | bytes 5898240 | tf_op jit(solution)/shard_map/attend_back/pallas_call | solution.py:160
  219.9 2.0 slice_add_fusion.1
  229.4 2.2 collective-permute-start.40
  231.6 12.7 %attend_back.3 = (bf16[1024,2304]{1,0:T(8,128)(2,1)S(1)}, f32[8,2304]{1,0:T(8,128)S(1)}) custom-call(s32[3]{0:T(128)S(1)} %pad_add_fusion.info_ref, bf16[1024,2304]{1,0:T(8,128)(2,1)S(1)} %bitcast.152, bf16[1024,2304]{1,0:T(8,128)(2,1)S(1)} %bitcast.152, bf16[1024,2304]{1,0:T(8,128)(2,1)S(1)} %bitcast.152, ...), custom_call_target="tpu_custom_call", output_to_operand_aliasing={{0}: (7, {})} | custom-call | flops 16000000000 | bytes 5898240 | tf_op jit(solution)/shard_map/attend_back/pallas_call | solution.py:160
  244.3 2.2 copy-done.31
  247.1 2.2 shares.1.refs_1_
  249.4 6.6 %convolution_convert_fusion.2.refs_0_ = bf16[768,2304]{1,0:T(8,128)(2,1)S(1)} fusion(bf16[1024,768]{1,0:T(8,128)(2,1)S(1)} %bitcast.146, bf16[1024,2304]{1,0:T(8,128)(2,1)} %copy-done.31), kind=kOutput, calls=%fused_computation.5 | convolution fusion | flops 3625648128 | bytes 9830400 | tf_op jit(solution)/shard_map/dot_general | solution.py:39
  259.9 2.0 slice_add_fusion
  267.2 2.1 collective-permute-done.46
  276.4 9.7 %collective-permute-done.49 = bf16[48,1536]{1,0:T(8,128)(2,1)S(1)} collective-permute-done((bf16[48,1536]{1,0:T(8,128)(2,1)}, bf16[48,1536]{1,0:T(8,128)(2,1)S(1)}, u32[]{:S(2)}, u32[]{:S(2)}) %collective-permute-start.49) | collective-permute-done | bytes 147488 | tf_op jit(solution)/shard_map/ppermute | solution.py:309
  289.7 2.3 collective-permute-start.54
  295.2 2.2 collective-permute-done.53
  297.3 4.7 %collective-permute-done.52 = bf16[4,160,384]{2,1,0:T(8,128)(2,1)S(1)} collective-permute-done((bf16[4,160,384]{2,1,0:T(8,128)(2,1)S(1)}, bf16[4,160,384]{2,1,0:T(8,128)(2,1)S(1)}, u32[]{:S(2)}, u32[]{:S(2)}) %collective-permute-start.52) | collective-permute-done | bytes 491552 | tf_op jit(solution)/shard_map/ppermute | solution.py:309
  306.6 2.5 collective-permute-start.58
  310.2 2.4 copy.36
  319.1 3.7 %copy.37 = f32[256,4,768]{2,1,0:T(4,128)} copy(f32[256,4,768]{2,0,1:T(8,128)S(1)} %maximum_bitcast_fusion) | data formatting | bytes 6291456
  (327 shorter events, 98.8 us)
Async XLA Ops:
  6.4 16.6 %collective-permute-start.3 = (bf16[1,256,768]{2,1,0:T(8,128)(2,1)S(1)}, bf16[1,256,768]{2,1,0:T(8,128)(2,1)S(1)}, u32[]{:S(2)}, u32[]{:S(2)}) collective-permute-start(bf16[1,256,768]{2,1,0:T(8,128)(2,1)S(1)} %slice.334), channel_id=1, source_target_pairs={{0,1},{1,0},{2,3},{3,2},{4,5},{5,4},{6,7},{7,6},{8,9},{9,8},{10,11... | collective-permute-start | bytes 1179656 | tf_op jit(solution)/shard_map/ppermute | solution.py:583
  11.0 12.0 %collective-permute-start.1 = (bf16[160,384]{1,0:T(8,128)(2,1)S(1)}, bf16[160,384]{1,0:T(8,128)(2,1)S(1)}, u32[]{:S(2)}, u32[]{:S(2)}) collective-permute-start(bf16[160,384]{1,0:T(8,128)(2,1)S(1)} %pad_maximum_fusion.9), channel_id=1, source_target_pairs={{0,16},{1,17},{2,18},{3,19},{4,20},{5,21},{6,22},{7,23},{8,24},{9,... | collective-permute-start | bytes 368648 | tf_op jit(solution)/shard_map/ppermute | solution.py:309
  13.6 9.4 %collective-permute-start.2 = (bf16[160,384]{1,0:T(8,128)(2,1)S(1)}, bf16[160,384]{1,0:T(8,128)(2,1)S(1)}, u32[]{:S(2)}, u32[]{:S(2)}) collective-permute-start(bf16[160,384]{1,0:T(8,128)(2,1)S(1)} %pad_maximum_fusion.9), channel_id=1, source_target_pairs={{0,24},{1,25},{2,26},{3,27},{4,28},{5,29},{6,30},{7,31},{8,16},{9,... | collective-permute-start | bytes 368648 | tf_op jit(solution)/shard_map/ppermute | solution.py:309
  23.1 19.3 %collective-permute-start.4 = (bf16[4,160,384]{2,1,0:T(8,128)(2,1)S(1)}, bf16[4,160,384]{2,1,0:T(8,128)(2,1)S(1)}, u32[]{:S(2)}, u32[]{:S(2)}) collective-permute-start(bf16[4,160,384]{2,1,0:T(8,128)(2,1)S(1)} %pad_maximum_fusion.5.refs_0_), channel_id=1, source_target_pairs={{0,4},{1,5},{2,3},{3,2},{4,0},{5,1},{6,7},{7,6},{8,12},{9,13},{10,... | collective-permute-start | bytes 1474568 | tf_op jit(solution)/shard_map/ppermute | solution.py:309
  24.6 17.7 %collective-permute-start.5 = (bf16[4,160,384]{2,1,0:T(8,128)(2,1)S(1)}, bf16[4,160,384]{2,1,0:T(8,128)(2,1)S(1)}, u32[]{:S(2)}, u32[]{:S(2)}) collective-permute-start(bf16[4,160,384]{2,1,0:T(8,128)(2,1)S(1)} %pad_maximum_fusion.5.refs_0_), channel_id=1, source_target_pairs={{0,1},{1,0},{2,6},{3,7},{4,5},{5,4},{6,2},{7,3},{8,9},{9,8},{10,14... | collective-permute-start | bytes 1474568 | tf_op jit(solution)/shard_map/ppermute | solution.py:309
  25.2 17.2 %collective-permute-start.8 = (bf16[1,256,768]{2,1,0:T(8,128)(2,1)S(1)}, bf16[1,256,768]{2,1,0:T(8,128)(2,1)S(1)}, u32[]{:S(2)}, u32[]{:S(2)}) collective-permute-start(bf16[1,256,768]{2,1,0:T(8,128)(2,1)S(1)} %slice.257), channel_id=1, source_target_pairs={{0,1},{1,0},{2,3},{3,2},{4,5},{5,4},{6,7},{7,6},{8,9},{9,8},{10,11... | collective-permute-start | bytes 1179656 | tf_op jit(solution)/shard_map/ppermute | solution.py:583
  26.8 15.6 %collective-permute-start.6 = (bf16[48,1920]{1,0:T(8,128)(2,1)S(1)}, bf16[48,1920]{1,0:T(8,128)(2,1)S(1)}, u32[]{:S(2)}, u32[]{:S(2)}) collective-permute-start(bf16[48,1920]{1,0:T(8,128)(2,1)S(1)} %pad_maximum_fusion.8), channel_id=1, source_target_pairs={{0,16},{1,17},{2,18},{3,19},{4,20},{5,21},{6,22},{7,23},{8,24},{9,... | collective-permute-start | bytes 552968 | tf_op jit(solution)/shard_map/ppermute | solution.py:309
  29.7 12.7 %collective-permute-start.7 = (bf16[48,1536]{1,0:T(8,128)(2,1)S(1)}, bf16[48,1536]{1,0:T(8,128)(2,1)S(1)}, u32[]{:S(2)}, u32[]{:S(2)}) collective-permute-start(bf16[48,1536]{1,0:T(8,128)(2,1)S(1)} %bitcast.162), channel_id=1, source_target_pairs={{0,16},{1,17},{2,18},{3,19},{4,20},{5,21},{6,22},{7,23},{8,24},{9,... | collective-permute-start | bytes 442376 | tf_op jit(solution)/shard_map/ppermute | solution.py:309
  42.4 9.4 %collective-permute-start.13 = (bf16[2,48,1920]{2,1,0:T(8,128)(2,1)S(1)}, bf16[2,48,1920]{2,1,0:T(8,128)(2,1)S(1)}, u32[]{:S(2)}, u32[]{:S(2)}) collective-permute-start(bf16[2,48,1920]{2,1,0:T(8,128)(2,1)S(1)} %pad_maximum_fusion.6), channel_id=1, source_target_pairs={{0,8},{1,9},{2,10},{3,11},{4,12},{5,13},{6,14},{7,15},{8,0},{9,1},... | collective-permute-start | bytes 1105928 | tf_op jit(solution)/shard_map/ppermute | solution.py:309
  45.3 9.0 %collective-permute-start.9 = (bf16[4,160,384]{2,1,0:T(8,128)(2,1)S(1)}, bf16[4,160,384]{2,1,0:T(8,128)(2,1)}, u32[]{:S(2)}, u32[]{:S(2)}) collective-permute-start(bf16[4,160,384]{2,1,0:T(8,128)(2,1)S(1)} %collective-permute-done.4.refs_1_), channel_id=1, source_target_pairs={{0,1},{1,0},{2,6},{3,7},{4,5},{5,4},{6,2},{7,3},{8,9},{9,8},{10,14... | collective-permute-start | bytes 1474568 | tf_op jit(solution)/shard_map/ppermute | solution.py:309
  55.9 9.6 %collective-permute-start.17 = (bf16[4,160,384]{2,1,0:T(8,128)(2,1)}, bf16[4,160,384]{2,1,0:T(8,128)(2,1)S(1)}, u32[]{:S(2)}, u32[]{:S(2)}) collective-permute-start(bf16[4,160,384]{2,1,0:T(8,128)(2,1)} %collective-permute-done.9.refs_3_), channel_id=1, source_target_pairs={{0,2},{1,3},{2,0},{3,1},{4,6},{5,7},{6,4},{7,5},{8,10},{9,11},{10,... | collective-permute-start | bytes 1474568 | tf_op jit(solution)/shard_map/ppermute | solution.py:309
  56.1 19.2 %collective-permute-start.14 = (bf16[4,48,1920]{2,1,0:T(8,128)(2,1)S(1)}, bf16[4,48,1920]{2,1,0:T(8,128)(2,1)S(1)}, u32[]{:S(2)}, u32[]{:S(2)}) collective-permute-start(bf16[4,48,1920]{2,1,0:T(8,128)(2,1)S(1)} %pad_maximum_fusion.3.refs_0_), channel_id=1, source_target_pairs={{0,4},{1,5},{2,3},{3,2},{4,0},{5,1},{6,7},{7,6},{8,12},{9,13},{10,... | collective-permute-start | bytes 2211848 | tf_op jit(solution)/shard_map/ppermute | solution.py:309
  57.7 17.6 %collective-permute-start.15 = (bf16[4,48,1920]{2,1,0:T(8,128)(2,1)S(1)}, bf16[4,48,1920]{2,1,0:T(8,128)(2,1)}, u32[]{:S(2)}, u32[]{:S(2)}) collective-permute-start(bf16[4,48,1920]{2,1,0:T(8,128)(2,1)S(1)} %pad_maximum_fusion.3.refs_0_), channel_id=1, source_target_pairs={{0,1},{1,0},{2,6},{3,7},{4,5},{5,4},{6,2},{7,3},{8,9},{9,8},{10,14... | collective-permute-start | bytes 2211848 | tf_op jit(solution)/shard_map/ppermute | solution.py:309
  58.2 17.1 %collective-permute-start.16 = (bf16[4,48,1920]{2,1,0:T(8,128)(2,1)S(1)}, bf16[4,48,1920]{2,1,0:T(8,128)(2,1)}, u32[]{:S(2)}, u32[]{:S(2)}) collective-permute-start(bf16[4,48,1920]{2,1,0:T(8,128)(2,1)S(1)} %pad_maximum_fusion.3.refs_0_), channel_id=1, source_target_pairs={{0,2},{1,3},{2,0},{3,1},{4,6},{5,7},{6,4},{7,5},{8,10},{9,11},{10,... | collective-permute-start | bytes 2211848 | tf_op jit(solution)/shard_map/ppermute | solution.py:309
  75.3 18.2 %collective-permute-start.18 = (bf16[4,48,1920]{2,1,0:T(8,128)(2,1)S(1)}, bf16[4,48,1920]{2,1,0:T(8,128)(2,1)S(1)}, u32[]{:S(2)}, u32[]{:S(2)}) collective-permute-start(bf16[4,48,1920]{2,1,0:T(8,128)(2,1)S(1)} %collective-permute-done.14.refs_1_), channel_id=1, source_target_pairs={{0,1},{1,0},{2,6},{3,7},{4,5},{5,4},{6,2},{7,3},{8,9},{9,8},{10,14... | collective-permute-start | bytes 2211848 | tf_op jit(solution)/shard_map/ppermute | solution.py:309
  75.7 17.8 %collective-permute-start.19 = (bf16[4,48,1920]{2,1,0:T(8,128)(2,1)S(1)}, bf16[4,48,1920]{2,1,0:T(8,128)(2,1)S(1)}, u32[]{:S(2)}, u32[]{:S(2)}) collective-permute-start(bf16[4,48,1920]{2,1,0:T(8,128)(2,1)S(1)} %collective-permute-done.14.refs_1_), channel_id=1, source_target_pairs={{0,2},{1,3},{2,0},{3,1},{4,6},{5,7},{6,4},{7,5},{8,10},{9,11},{10,... | collective-permute-start | bytes 2211848 | tf_op jit(solution)/shard_map/ppermute | solution.py:309
  82.9 21.2 %collective-permute-start.23 = (bf16[4,48,1536]{2,1,0:T(8,128)(2,1)S(1)}, bf16[4,48,1536]{2,1,0:T(8,128)(2,1)S(1)}, u32[]{:S(2)}, u32[]{:S(2)}) collective-permute-start(bf16[4,48,1536]{2,1,0:T(8,128)(2,1)S(1)} %pad_maximum_fusion.4.refs_0_), channel_id=1, source_target_pairs={{0,4},{1,5},{2,3},{3,2},{4,0},{5,1},{6,7},{7,6},{8,12},{9,13},{10,... | collective-permute-start | bytes 1769480 | tf_op jit(solution)/shard_map/ppermute | solution.py:309
  83.6 20.5 %collective-permute-start.24 = (bf16[4,48,1536]{2,1,0:T(8,128)(2,1)S(1)}, bf16[4,48,1536]{2,1,0:T(8,128)(2,1)S(1)}, u32[]{:S(2)}, u32[]{:S(2)}) collective-permute-start(bf16[4,48,1536]{2,1,0:T(8,128)(2,1)S(1)} %pad_maximum_fusion.4.refs_0_), channel_id=1, source_target_pairs={{0,1},{1,0},{2,6},{3,7},{4,5},{5,4},{6,2},{7,3},{8,9},{9,8},{10,14... | collective-permute-start | bytes 1769480 | tf_op jit(solution)/shard_map/ppermute | solution.py:309
  93.6 10.5 %collective-permute-start.22 = (bf16[4,48,1920]{2,1,0:T(8,128)(2,1)S(1)}, bf16[4,48,1920]{2,1,0:T(8,128)(2,1)S(1)}, u32[]{:S(2)}, u32[]{:S(2)}) collective-permute-start(bf16[4,48,1920]{2,1,0:T(8,128)(2,1)S(1)} %collective-permute-done.18.refs_3_), channel_id=1, source_target_pairs={{0,2},{1,3},{2,0},{3,1},{4,6},{5,7},{6,4},{7,5},{8,10},{9,11},{10,... | collective-permute-start | bytes 2211848 | tf_op jit(solution)/shard_map/ppermute | solution.py:309
  104.1 17.2 %collective-permute-start.25 = (bf16[4,48,1536]{2,1,0:T(8,128)(2,1)S(1)}, bf16[4,48,1536]{2,1,0:T(8,128)(2,1)S(1)}, u32[]{:S(2)}, u32[]{:S(2)}) collective-permute-start(bf16[4,48,1536]{2,1,0:T(8,128)(2,1)S(1)} %collective-permute-done.23.refs_1_), channel_id=1, source_target_pairs={{0,1},{1,0},{2,6},{3,7},{4,5},{5,4},{6,2},{7,3},{8,9},{9,8},{10,14... | collective-permute-start | bytes 1769480 | tf_op jit(solution)/shard_map/ppermute | solution.py:309
  104.6 16.8 %collective-permute-start.27 = (bf16[4,48,1536]{2,1,0:T(8,128)(2,1)S(1)}, bf16[4,48,1536]{2,1,0:T(8,128)(2,1)S(1)}, u32[]{:S(2)}, u32[]{:S(2)}) collective-permute-start(bf16[4,48,1536]{2,1,0:T(8,128)(2,1)S(1)} %collective-permute-done.23.refs_1_), channel_id=1, source_target_pairs={{0,2},{1,3},{2,0},{3,1},{4,6},{5,7},{6,4},{7,5},{8,10},{9,11},{10,... | collective-permute-start | bytes 1769480 | tf_op jit(solution)/shard_map/ppermute | solution.py:309
  104.6 16.8 %collective-permute-start.26 = (bf16[4,48,1536]{2,1,0:T(8,128)(2,1)S(1)}, bf16[4,48,1536]{2,1,0:T(8,128)(2,1)S(1)}, u32[]{:S(2)}, u32[]{:S(2)}) collective-permute-start(bf16[4,48,1536]{2,1,0:T(8,128)(2,1)S(1)} %pad_maximum_fusion.4.refs_0_), channel_id=1, source_target_pairs={{0,2},{1,3},{2,0},{3,1},{4,6},{5,7},{6,4},{7,5},{8,10},{9,11},{10,... | collective-permute-start | bytes 1769480 | tf_op jit(solution)/shard_map/ppermute | solution.py:309
  105.1 16.3 %collective-permute-start.28 = (bf16[4,48,1536]{2,1,0:T(8,128)(2,1)S(1)}, bf16[4,48,1536]{2,1,0:T(8,128)(2,1)S(1)}, u32[]{:S(2)}, u32[]{:S(2)}) collective-permute-start(bf16[4,48,1536]{2,1,0:T(8,128)(2,1)S(1)} %collective-permute-done.24.refs_2_), channel_id=1, source_target_pairs={{0,2},{1,3},{2,0},{3,1},{4,6},{5,7},{6,4},{7,5},{8,10},{9,11},{10,... | collective-permute-start | bytes 1769480 | tf_op jit(solution)/shard_map/ppermute | solution.py:309
  105.4 25.5 %collective-permute-start.30 = (bf16[2,256,768]{2,1,0:T(8,128)(2,1)S(1)}, bf16[2,256,768]{2,1,0:T(8,128)(2,1)S(1)}, u32[]{:S(2)}, u32[]{:S(2)}) collective-permute-start(bf16[2,256,768]{2,1,0:T(8,128)(2,1)S(1)} %get-tuple-element.466), channel_id=1, source_target_pairs={{0,1},{1,0},{2,3},{3,2},{4,5},{5,4},{6,7},{7,6},{8,9},{9,8},{10,11... | collective-permute-start | bytes 2359304 | tf_op jit(solution)/shard_map/ppermute | solution.py:583
  121.3 9.6 %collective-permute-start.29 = (bf16[4,48,1536]{2,1,0:T(8,128)(2,1)S(1)}, bf16[4,48,1536]{2,1,0:T(8,128)(2,1)S(1)}, u32[]{:S(2)}, u32[]{:S(2)}) collective-permute-start(bf16[4,48,1536]{2,1,0:T(8,128)(2,1)S(1)} %collective-permute-done.25.refs_3_), channel_id=1, source_target_pairs={{0,2},{1,3},{2,0},{3,1},{4,6},{5,7},{6,4},{7,5},{8,10},{9,11},{10,... | collective-permute-start | bytes 1769480 | tf_op jit(solution)/shard_map/ppermute | solution.py:309
  145.8 11.4 %collective-permute-start.31 = (bf16[1,256,768]{2,1,0:T(8,128)(2,1)S(1)}, bf16[1,256,768]{2,1,0:T(8,128)(2,1)S(1)}, u32[]{:S(2)}, u32[]{:S(2)}) collective-permute-start(bf16[1,256,768]{2,1,0:T(8,128)(2,1)S(1)} %get-tuple-element.325), channel_id=1, source_target_pairs={{0,1},{1,0},{2,3},{3,2},{4,5},{5,4},{6,7},{7,6},{8,9},{9,8},{10,11... | collective-permute-start | bytes 1179656 | tf_op jit(solution)/shard_map/ppermute | solution.py:583
  157.2 11.5 %collective-permute-start.32 = (bf16[4,4,48,1536]{3,2,1,0:T(8,128)(2,1)S(1)}, bf16[4,4,48,1536]{3,2,1,0:T(8,128)(2,1)}, u32[]{:S(2)}, u32[]{:S(2)}) collective-permute-start(bf16[4,4,48,1536]{3,2,1,0:T(8,128)(2,1)S(1)} %get-tuple-element.328), channel_id=1, source_target_pairs={{0,2},{1,3},{2,0},{3,1},{4,6},{5,7},{6,4},{7,5},{8,10},{9,11},{10,... | collective-permute-start | bytes 7077896 | tf_op jit(solution)/shard_map/ppermute | solution.py:309
  157.2 11.5 %collective-permute-start.33 = (bf16[1,256,768]{2,1,0:T(8,128)(2,1)S(1)}, bf16[1,256,768]{2,1,0:T(8,128)(2,1)S(1)}, u32[]{:S(2)}, u32[]{:S(2)}) collective-permute-start(bf16[1,256,768]{2,1,0:T(8,128)(2,1)S(1)} %get-tuple-element.331), channel_id=1, source_target_pairs={{0,1},{1,0},{2,3},{3,2},{4,5},{5,4},{6,7},{7,6},{8,9},{9,8},{10,11... | collective-permute-start | bytes 1179656 | tf_op jit(solution)/shard_map/ppermute | solution.py:583
  175.7 22.2 %collective-permute-start.36 = (bf16[4,4,48,1536]{3,2,1,0:T(8,128)(2,1)S(1)}, bf16[4,4,48,1536]{3,2,1,0:T(8,128)(2,1)}, u32[]{:S(2)}, u32[]{:S(2)}) collective-permute-start(bf16[4,4,48,1536]{3,2,1,0:T(8,128)(2,1)S(1)} %get-tuple-element.338), channel_id=1, source_target_pairs={{0,2},{1,3},{2,0},{3,1},{4,6},{5,7},{6,4},{7,5},{8,10},{9,11},{10,... | collective-permute-start | bytes 7077896 | tf_op jit(solution)/shard_map/ppermute | solution.py:309
  179.2 18.7 %collective-permute-start.34 = (bf16[4,48,1536]{2,1,0:T(8,128)(2,1)}, bf16[4,48,1536]{2,1,0:T(8,128)(2,1)}, u32[]{:S(2)}, u32[]{:S(2)}) collective-permute-start(bf16[4,48,1536]{2,1,0:T(8,128)(2,1)} %get-tuple-element.453), channel_id=1, source_target_pairs={{0,1},{1,0},{2,6},{3,7},{4,5},{5,4},{6,2},{7,3},{8,9},{9,8},{10,14... | collective-permute-start | bytes 1769480 | tf_op jit(solution)/shard_map/ppermute | solution.py:309
  179.6 18.3 %collective-permute-start.35 = (bf16[4,48,1536]{2,1,0:T(8,128)(2,1)}, bf16[4,48,1536]{2,1,0:T(8,128)(2,1)}, u32[]{:S(2)}, u32[]{:S(2)}) collective-permute-start(bf16[4,48,1536]{2,1,0:T(8,128)(2,1)} %get-tuple-element.452), channel_id=1, source_target_pairs={{0,1},{1,0},{2,6},{3,7},{4,5},{5,4},{6,2},{7,3},{8,9},{9,8},{10,14... | collective-permute-start | bytes 1769480 | tf_op jit(solution)/shard_map/ppermute | solution.py:309
  201.3 17.0 %collective-permute-start.38 = (bf16[4,48,1536]{2,1,0:T(8,128)(2,1)S(1)}, bf16[4,48,1536]{2,1,0:T(8,128)(2,1)S(1)}, u32[]{:S(2)}, u32[]{:S(2)}) collective-permute-start(bf16[4,48,1536]{2,1,0:T(8,128)(2,1)S(1)} %get-tuple-element.449), channel_id=1, source_target_pairs={{0,1},{1,0},{2,6},{3,7},{4,5},{5,4},{6,2},{7,3},{8,9},{9,8},{10,14... | collective-permute-start | bytes 1769480 | tf_op jit(solution)/shard_map/ppermute | solution.py:309
  202.0 16.3 %collective-permute-start.39 = (bf16[4,4,48,384]{3,2,1,0:T(8,128)(2,1)S(1)}, bf16[4,4,48,384]{3,2,1,0:T(8,128)(2,1)S(1)}, u32[]{:S(2)}, u32[]{:S(2)}) collective-permute-start(bf16[4,4,48,384]{3,2,1,0:T(8,128)(2,1)S(1)} %get-tuple-element.352), channel_id=1, source_target_pairs={{0,2},{1,3},{2,0},{3,1},{4,6},{5,7},{6,4},{7,5},{8,10},{9,11},{10,... | collective-permute-start | bytes 1769480 | tf_op jit(solution)/shard_map/ppermute | solution.py:309
  203.6 16.3 %collective-permute-start.37 = (bf16[4,48,1536]{2,1,0:T(8,128)(2,1)S(1)}, bf16[4,48,1536]{2,1,0:T(8,128)(2,1)S(1)}, u32[]{:S(2)}, u32[]{:S(2)}) collective-permute-start(bf16[4,48,1536]{2,1,0:T(8,128)(2,1)S(1)} %add_convert_fusion.8), channel_id=1, source_target_pairs={{0,4},{1,5},{2,3},{3,2},{4,0},{5,1},{6,7},{7,6},{8,12},{9,13},{10,... | collective-permute-start | bytes 1769480 | tf_op jit(solution)/shard_map/ppermute | solution.py:309
  205.0 44.3 %collective-permute-start.41 = (bf16[4,48,1536]{2,1,0:T(8,128)(2,1)}, bf16[4,48,1536]{2,1,0:T(8,128)(2,1)}, u32[]{:S(2)}, u32[]{:S(2)}) collective-permute-start(bf16[4,48,1536]{2,1,0:T(8,128)(2,1)} %get-tuple-element.448), channel_id=1, source_target_pairs={{0,1},{1,0},{2,6},{3,7},{4,5},{5,4},{6,2},{7,3},{8,9},{9,8},{10,14... | collective-permute-start | bytes 1769480 | tf_op jit(solution)/shard_map/ppermute | solution.py:309
  222.8 26.6 %collective-permute-start.44 = (bf16[256,768]{1,0:T(8,128)(2,1)}, bf16[256,768]{1,0:T(8,128)(2,1)}, u32[]{:S(2)}, u32[]{:S(2)}) collective-permute-start(bf16[256,768]{1,0:T(8,128)(2,1)} %slice.439), channel_id=1, source_target_pairs={{0,1},{1,0},{2,3},{3,2},{4,5},{5,4},{6,7},{7,6},{8,9},{9,8},{10,11... | collective-permute-start | bytes 1179656 | tf_op jit(solution)/shard_map/ppermute | solution.py:583
  225.3 24.0 %collective-permute-start.42 = (bf16[4,48,384]{2,1,0:T(8,128)(2,1)}, bf16[4,48,384]{2,1,0:T(8,128)(2,1)}, u32[]{:S(2)}, u32[]{:S(2)}) collective-permute-start(bf16[4,48,384]{2,1,0:T(8,128)(2,1)} %get-tuple-element.471), channel_id=1, source_target_pairs={{0,1},{1,0},{2,6},{3,7},{4,5},{5,4},{6,2},{7,3},{8,9},{9,8},{10,14... | collective-permute-start | bytes 442376 | tf_op jit(solution)/shard_map/ppermute | solution.py:309
  225.7 23.6 %collective-permute-start.43 = (bf16[4,48,384]{2,1,0:T(8,128)(2,1)}, bf16[4,48,384]{2,1,0:T(8,128)(2,1)}, u32[]{:S(2)}, u32[]{:S(2)}) collective-permute-start(bf16[4,48,384]{2,1,0:T(8,128)(2,1)} %get-tuple-element.470), channel_id=1, source_target_pairs={{0,1},{1,0},{2,6},{3,7},{4,5},{5,4},{6,2},{7,3},{8,9},{9,8},{10,14... | collective-permute-start | bytes 442376 | tf_op jit(solution)/shard_map/ppermute | solution.py:309
  229.4 19.9 %collective-permute-start.40 = (bf16[2,48,1536]{2,1,0:T(8,128)(2,1)}, bf16[2,48,1536]{2,1,0:T(8,128)(2,1)}, u32[]{:S(2)}, u32[]{:S(2)}) collective-permute-start(bf16[2,48,1536]{2,1,0:T(8,128)(2,1)} %get-tuple-element.476), channel_id=1, source_target_pairs={{0,16},{1,17},{2,18},{3,19},{4,20},{5,21},{6,22},{7,23},{8,24},{9,... | collective-permute-start | bytes 884744 | tf_op jit(solution)/shard_map/ppermute | solution.py:309
  257.5 11.8 %collective-permute-start.45 = (bf16[4,4,160,384]{3,2,1,0:T(8,128)(2,1)S(1)}, bf16[4,4,160,384]{3,2,1,0:T(8,128)(2,1)S(1)}, u32[]{:S(2)}, u32[]{:S(2)}) collective-permute-start(bf16[4,4,160,384]{3,2,1,0:T(8,128)(2,1)S(1)} %get-tuple-element.378), channel_id=1, source_target_pairs={{0,2},{1,3},{2,0},{3,1},{4,6},{5,7},{6,4},{7,5},{8,10},{9,11},{10,... | collective-permute-start | bytes 5898248 | tf_op jit(solution)/shard_map/ppermute | solution.py:309
  259.3 9.9 %collective-permute-start.46 = (bf16[4,48,1536]{2,1,0:T(8,128)(2,1)S(1)}, bf16[4,48,1536]{2,1,0:T(8,128)(2,1)S(1)}, u32[]{:S(2)}, u32[]{:S(2)}) collective-permute-start(bf16[4,48,1536]{2,1,0:T(8,128)(2,1)S(1)} %add_convert_fusion.2), channel_id=1, source_target_pairs={{0,4},{1,5},{2,3},{3,2},{4,0},{5,1},{6,7},{7,6},{8,12},{9,13},{10,... | collective-permute-start | bytes 1769480 | tf_op jit(solution)/shard_map/ppermute | solution.py:309
  264.6 11.8 %collective-permute-start.51 = (bf16[4,48,384]{2,1,0:T(8,128)(2,1)}, bf16[4,48,384]{2,1,0:T(8,128)(2,1)}, u32[]{:S(2)}, u32[]{:S(2)}) collective-permute-start(bf16[4,48,384]{2,1,0:T(8,128)(2,1)} %add_convert_fusion.22), channel_id=1, source_target_pairs={{0,4},{1,5},{2,3},{3,2},{4,0},{5,1},{6,7},{7,6},{8,12},{9,13},{10,... | collective-permute-start | bytes 442376 | tf_op jit(solution)/shard_map/ppermute | solution.py:309
  270.3 15.8 %collective-permute-start.50 = (bf16[2,48,1536]{2,1,0:T(8,128)(2,1)}, bf16[2,48,1536]{2,1,0:T(8,128)(2,1)S(1)}, u32[]{:S(2)}, u32[]{:S(2)}) collective-permute-start(bf16[2,48,1536]{2,1,0:T(8,128)(2,1)} %get-tuple-element.474), channel_id=1, source_target_pairs={{0,16},{1,17},{2,18},{3,19},{4,20},{5,21},{6,22},{7,23},{8,24},{9,... | collective-permute-start | bytes 884744 | tf_op jit(solution)/shard_map/ppermute | solution.py:309
  272.4 13.7 %collective-permute-start.47 = (bf16[4,160,384]{2,1,0:T(8,128)(2,1)}, bf16[4,160,384]{2,1,0:T(8,128)(2,1)}, u32[]{:S(2)}, u32[]{:S(2)}) collective-permute-start(bf16[4,160,384]{2,1,0:T(8,128)(2,1)} %get-tuple-element.457), channel_id=1, source_target_pairs={{0,1},{1,0},{2,6},{3,7},{4,5},{5,4},{6,2},{7,3},{8,9},{9,8},{10,14... | collective-permute-start | bytes 1474568 | tf_op jit(solution)/shard_map/ppermute | solution.py:309
  272.8 13.9 %collective-permute-start.48 = (bf16[4,160,384]{2,1,0:T(8,128)(2,1)}, bf16[4,160,384]{2,1,0:T(8,128)(2,1)S(1)}, u32[]{:S(2)}, u32[]{:S(2)}) collective-permute-start(bf16[4,160,384]{2,1,0:T(8,128)(2,1)} %get-tuple-element.456), channel_id=1, source_target_pairs={{0,1},{1,0},{2,6},{3,7},{4,5},{5,4},{6,2},{7,3},{8,9},{9,8},{10,14... | collective-permute-start | bytes 1474568 | tf_op jit(solution)/shard_map/ppermute | solution.py:309
  275.2 10.9 %collective-permute-start.49 = (bf16[48,1536]{1,0:T(8,128)(2,1)}, bf16[48,1536]{1,0:T(8,128)(2,1)S(1)}, u32[]{:S(2)}, u32[]{:S(2)}) collective-permute-start(bf16[48,1536]{1,0:T(8,128)(2,1)} %get-tuple-element.485), channel_id=1, source_target_pairs={{0,8},{1,9},{2,10},{3,11},{4,12},{5,13},{6,14},{7,15},{8,0},{9,1},... | collective-permute-start | bytes 442376 | tf_op jit(solution)/shard_map/ppermute | solution.py:309
  293.1 8.9 %collective-permute-start.52 = (bf16[4,160,384]{2,1,0:T(8,128)(2,1)S(1)}, bf16[4,160,384]{2,1,0:T(8,128)(2,1)S(1)}, u32[]{:S(2)}, u32[]{:S(2)}) collective-permute-start(bf16[4,160,384]{2,1,0:T(8,128)(2,1)S(1)} %add_convert_fusion.14), channel_id=1, source_target_pairs={{0,4},{1,5},{2,3},{3,2},{4,0},{5,1},{6,7},{7,6},{8,12},{9,13},{10,... | collective-permute-start | bytes 1474568 | tf_op jit(solution)/shard_map/ppermute | solution.py:309
  302.1 10.5 %collective-permute-start.59 = (bf16[48,384]{1,0:T(8,128)(2,1)S(1)}, bf16[48,384]{1,0:T(8,128)(2,1)S(1)}, u32[]{:S(2)}, u32[]{:S(2)}) collective-permute-start(bf16[48,384]{1,0:T(8,128)(2,1)S(1)} %slice_bitcast_fusion.14), channel_id=1, source_target_pairs={{0,8},{1,9},{2,10},{3,11},{4,12},{5,13},{6,14},{7,15},{8,0},{9,1},... | collective-permute-start | bytes 110600 | tf_op jit(solution)/shard_map/ppermute | solution.py:309
  (87 other events, 575.4 us)
where the time goes:
time: 327 us; the launch traced here: 323 us
  Pallas kernels  90.6 us (28%)
  waiting for transfers between devices  63.8 us (20%)
  starting transfers between devices  56 us (17%)
  local copies, waits for them, and re-layouts  44.5 us (14%)
  matrix products  37.7 us (12%)
  other arithmetic  28.2 us (9%)
    ppermute x53, waiting for transfers between devices, swap(): return lax.ppermute(value, BOTH, pairs)  54.9 us
    ppermute x53, starting transfers between devices, swap(): return lax.ppermute(value, BOTH, pairs)  46.8 us
    unnamed x149, local copies, waits for them, and re-layouts  29.2 us
    pallas_call x2, Pallas kernels, attend_back(): pl.pallas_call(functools.partial(attend_back_kernel, seq=seq), grid_spec=...  25.1 us
    pallas_call x3, Pallas kernels, by_rows(): pl.pallas_call(kernel, grid=(rows // step,), in_specs=[spec(value.shape,...  19.3 us
    convert_element_type x15, other arithmetic, add_low(): return sum((part.astype(f32) for part in parts)).astype(bf16)  19.1 us
    dot_general x4, matrix products, dot_tn(): lax.dot_general(left, right, (((0,), (0,)), ((), ())), preferred_element_...  18.9 us
    pallas_call x2, Pallas kernels, attend(): pl.pallas_call(functools.partial(attend_kernel, seq=seq), grid_spec=pltpu...  16.4 us
  transfers between devices with their start and end apart: 60, of which 17 were waited for; matrix products, arithmetic and copies ran while one was open for 18% of the time, Pallas kernels for 24%

commit v1 on v0

--- a/solution.py
+++ b/solution.py
@@ -304,6 +304,30 @@
     )(*[value for value, _ in ins])
 
 
+def interleave_kernel(own_ref, *refs):
+    out_ref, seqs = refs[-1], len(refs) // 2
+    is_first = own_ref[0] == 0
+    for seq in range(seqs):
+        kept, got = refs[2 * seq][...], refs[2 * seq + 1][...].astype(f32)
+        out_ref[:, seq, :] = jnp.where(is_first, kept, got)
+        out_ref[:, seqs + seq, :] = jnp.where(is_first, got, kept)
+
+
+def interleave(own, halves):
+    count, width = halves[0][0].shape
+    step = 64
+    block = pl.BlockSpec((step, width), lambda i: (i, 0))
+    return pl.pallas_call(
+        interleave_kernel,
+        grid=(count // step,),
+        in_specs=[pl.BlockSpec(memory_space=pltpu.SMEM)] + [block] * (2 * len(halves)),
+        out_specs=pl.BlockSpec((step, 2 * len(halves), width), lambda i: (i, 0, 0)),
+        out_shape=jax.ShapeDtypeStruct((count, 2 * len(halves), width), f32),
+        compiler_params=pltpu.CompilerParams(vmem_limit_bytes=16 << 20),
+        name="interleave",
+    )(own, *[value for pair in halves for value in pair])
+
+
 def swap(value, even, odd):
     pairs = [(i, i ^ (odd if i & BIT_CORE else even)) for i in range(PLACES)]
     return lax.ppermute(value, BOTH, pairs)
@@ -390,25 +414,29 @@
     )(me, *wholes)
 
 
-def lines_kernel(v_ref, lines_ref, b_ref, *, count, wide):
+def lines_kernel(v_ref, qkv_ref, one_ref, two_ref, b_ref, *, count, wide):
     places = v_ref.shape[0] // 16
+    width = places * count
+    qkv_ref[:, width : 2 * width] = jnp.zeros((1, width), f32)
     for place in range(places):
         line = v_ref[pl.ds(place * 16, 16), :].astype(f32)[0:1]
         to = (place % 2) * (places // 2) + place // 2
-        starts = [0, count] + [2 * count + wide + i * count for i in range(6)]
-        for i, start in enumerate(starts):
-            lines_ref[i : i + 1, to * count : (to + 1) * count] = line[:, start : start + count]
+        qkv_ref[:, to * count : (to + 1) * count] = line[:, :count]
+        at = 2 * width + to * count
+        qkv_ref[:, at : at + count] = line[:, count : 2 * count]
         b_ref[:, to * wide : (to + 1) * wide] = line[:, 2 * count : 2 * count + wide]
+        lines = ((one_ref, 0), (two_ref, 0), (one_ref, 1), (one_ref, 2), (two_ref, 1), (two_ref, 2))
+        for i, (ref, at) in enumerate(lines):
+            start = 2 * count + wide + i * count
+            ref[at : at + 1, to * count : (to + 1) * count] = line[:, start : start + count]
 
 
 def unpack_lines(vector_rows, count, wide):
     places = vector_rows.shape[0] // 16
+    shapes = [(1, 3 * places * count), (3, places * count), (3, places * count), (1, places * wide)]
     return pl.pallas_call(
         functools.partial(lines_kernel, count=count, wide=wide),
-        out_shape=[
-            jax.ShapeDtypeStruct((8, places * count), f32),
-            jax.ShapeDtypeStruct((1, places * wide), f32),
-        ],
+        out_shape=[jax.ShapeDtypeStruct(shape, f32) for shape in shapes],
         name="lines",
     )(vector_rows)
 
@@ -639,8 +667,7 @@
     wq, vector_rows = attn.whole()
     wide = b_in.shape[0]
     if direct:
-        lines, b_in_all = unpack_lines(vector_rows, count, wide)
-        bias_pair, gains, shifts = lines[:2], lines[2:4], lines[4:]
+        qkv_shift, one_lines, two_lines, b_in_all = unpack_lines(vector_rows, count, wide)
     else:
         flat = vector_rows.reshape(places // 2, 2, 16, local_width)[:, :, 0]
         flat = jnp.swapaxes(flat, 0, 1).reshape(places, local_width).astype(f32)
@@ -651,13 +678,16 @@
 
         bias_pair, b_in_all = vector(0, 2, count), vector(2 * count, 1, wide)
         gains, shifts = vector(2 * count + wide, 2, count), vector(4 * count + wide, 4, count)
+        middle = jnp.zeros((width,), f32)
+        qkv_shift = jnp.concatenate([bias_pair[0], middle, bias_pair[1]])[None]
+        one_lines = jnp.stack([gains[0], shifts[0], shifts[1]])
+        two_lines = jnp.stack([gains[1], shifts[2], shifts[3]])
 
     mine_lengths = lax.dynamic_slice_in_dim(lengths, own * seqs, seqs, 0)
     info = jnp.concatenate([own.reshape(1).astype(jnp.int32), mine_lengths])
 
-    upper.held, wq, bias_pair = sync(upper.held, wq, bias_pair)
+    upper.held, wq, qkv_shift = sync(upper.held, wq, qkv_shift)
     upper.step()
-    qkv_shift = jnp.concatenate([bias_pair[0], jnp.zeros((width,), f32), bias_pair[1]])
     qkv = (dot(rows, wq) + qkv_shift).astype(bf16)
     lower.held, qkv = sync(lower.held, qkv)
     lower.step()
@@ -671,8 +701,6 @@
     lower.step()
     grad_halves = to_rows(cotangent)
     wi, wo = upper.whole()
-    one_lines = jnp.stack([gains[0], shifts[0], shifts[1]])
-    two_lines = jnp.stack([gains[1], shifts[2], shifts[3]])
     wide_rows = (total_rows, width)
     first, first_low, normed_one, inverse_one = by_rows(
         out_kernel,
@@ -714,16 +742,25 @@
         ],
     )
     by_half = output.reshape(seqs, 2, half_len, width)
-    early, late, mixed_grad, hidden = sync(by_half[:1, 1], by_half[1:, 1], mixed_grad, hidden)
-    early = trade(early)
+    part_rows = seqs * half_len // 4
+    sent_parts = by_half[:, 1].reshape(4, part_rows, width)
+    sent_parts, mixed_grad, hidden = sync(
+        [sent_parts[i] for i in range(4)], mixed_grad, hidden
+    )
+    out_parts = [trade(sent_parts[0])]
     grad_wd = dot_tn(mixed_grad, hidden).astype(bf16)
     down = Reduce(me, [grad_wd], mlp_moves, row, local_units, direct, folded=True)
-    down.held, mixed_grad, early, late = sync(down.held, mixed_grad, early, late)
-    late = trade(late)
+    down.held, mixed_grad, out_parts, sent_parts = sync(
+        down.held, mixed_grad, out_parts, sent_parts
+    )
+    out_parts.append(trade(sent_parts[1]))
     down.step()
     grad_before = (dot(mixed_grad, wd) * slope.astype(f32)).astype(bf16)
-    down.held, grad_before, late = sync(down.held, grad_before, late)
+    down.held, grad_before, out_parts, sent_parts = sync(
+        down.held, grad_before, out_parts, sent_parts
+    )
     down.step()
+    out_parts.append(trade(sent_parts[2]))
     grad_in_bias = jnp.sum(grad_before, axis=0, dtype=f32)
     grad_wi = dot_tn(first_low, grad_before).astype(bf16)
     into = Reduce(me, [grad_wi], mlp_moves, row, local_units, direct, folded=True)
@@ -746,7 +783,9 @@
     )
     grad_wo = dot_tn(attn_grad, ctx).astype(bf16)
     grad_ctx = dot(attn_grad, wo).astype(bf16)
-    down.held, into.held, grad_wo, grad_ctx = sync(down.held, into.held, grad_wo, grad_ctx)
+    down.held, into.held, grad_wo, grad_ctx, out_parts = sync(
+        down.held, into.held, grad_wo, grad_ctx, out_parts
+    )
     down.step()
     into.step()
     outer = Reduce(me, [grad_wo], out_moves, row, local_width, direct, folded=True)
@@ -778,6 +817,7 @@
         down.held, into.held, outer.held, token_halves, grad_triple
     )
     into.step()
+    out_parts.append(trade(sent_parts[3]))
     grad_wq = dot_tn(rows, grad_triple).astype(bf16)
 
     if direct:
@@ -797,6 +837,7 @@
         grad_vectors = pack(
             [shares(grad_pair, 2), shares(grad_in_bias, 1), shares(jnp.stack(grad_lines), 6)], bf16
         ).reshape(places * 16, local_width)
+    grad_wq, out_parts = sync(grad_wq, out_parts)
     triple = Reduce(
         me, [grad_wq, grad_vectors], qkv_moves, 3 * row + 16, local_width, direct
     )
@@ -808,24 +849,23 @@
     into.step()
     down.step()
     outer.step()
-    triple.held, down.held, into.held, outer.held, early, late, by_half = sync(
-        triple.held, down.held, into.held, outer.held, early, late, by_half
+    triple.held, down.held, into.held, outer.held, out_parts, by_half, sent = sync(
+        triple.held, down.held, into.held, outer.held, out_parts, by_half, sent
     )
     triple.step()
     into.step()
     outer.step()
-    out = from_rows(by_half[:, 0], jnp.concatenate([early, late]), bf16)
+    out = from_rows(
+        by_half[:, 0], jnp.stack(out_parts).reshape(seqs, half_len, width), bf16
+    )
     triple.held, into.held, outer.held, sent, out = sync(
         triple.held, into.held, outer.held, sent, out
     )
     triple.step()
     outer.step()
     token_halves.append([kept, trade(sent)])
-    d_tokens = from_rows(
-        jnp.stack([kept for kept, _ in token_halves]),
-        jnp.stack([got for _, got in token_halves]).astype(f32),
-        f32,
-    )
+    d_tokens = interleave(own.reshape(1).astype(jnp.int32), token_halves)
+    triple.held, d_tokens = sync(triple.held, d_tokens)
     grad_down = down.shard().T
     grad_in = into.shard()
     grad_out = outer.shard().T

time: 327 us -> 325 us (level)
  local copies, waits for them, and re-layouts: 44.5 us -> 37.4 us
  waiting for transfers between devices: 63.8 us -> 58.1 us
  Pallas kernels: 90.6 us -> 94.1 us
  starting transfers between devices: 56 us -> 59.3 us
    unnamed x149 -> x141, local copies, waits for them, and re-layouts: 29.2 us -> 22.1 us
    ppermute x7 -> x9, waiting for transfers between devices: 8.94 us -> 4.08 us  [trade(): return lax.ppermute(value, 'tensor', [(0, 1), (1, 0)])]
    ppermute x7 -> x9, starting transfers between devices: 9.21 us -> 12.4 us  [trade(): return lax.ppermute(value, 'tensor', [(0, 1), (1, 0)])]
  transfers between devices with their start and end apart: 60 -> 62, of which waited for: 17 -> 13; matrix products, arithmetic and copies ran while one was open for 18% -> 21% of each run, Pallas kernels for 24% -> 25%
where the time goes in v1:
time: 325 us; the launch traced here: 321 us
  Pallas kernels  94.1 us (29%)
  starting transfers between devices  59.3 us (18%)
  waiting for transfers between devices  58.1 us (18%)
  matrix products  39.6 us (12%)
  local copies, waits for them, and re-layouts  37.4 us (12%)
  other arithmetic  30.7 us (9%)
    ppermute x53, waiting for transfers between devices, swap(): return lax.ppermute(value, BOTH, pairs)  54 us
    ppermute x53, starting transfers between devices, swap(): return lax.ppermute(value, BOTH, pairs)  46.9 us
    pallas_call x2, Pallas kernels, attend_back(): pl.pallas_call(functools.partial(attend_back_kernel, seq=seq), grid_spec=...  25.4 us
    unnamed x141, local copies, waits for them, and re-layouts  22.1 us
    dot_general x4, matrix products, dot_tn(): lax.dot_general(left, right, (((0,), (0,)), ((), ())), preferred_element_...  20.3 us
    pallas_call x3, Pallas kernels, by_rows(): pl.pallas_call(kernel, grid=(rows // step,), in_specs=[spec(value.shape,...  19.9 us
    convert_element_type x15, other arithmetic, add_low(): return sum((part.astype(f32) for part in parts)).astype(bf16)  18.9 us
    pallas_call x2, Pallas kernels, attend(): pl.pallas_call(functools.partial(attend_kernel, seq=seq), grid_spec=pltpu...  16.4 us
  transfers between devices with their start and end apart: 62, of which 13 were waited for; matrix products, arithmetic and copies ran while one was open for 21% of the time, Pallas kernels for 25%

profile of v1, /device:TPU:0, one launch (start us, length us, event | category | flops | bytes accessed | tf_op | source)
XLA Modules:
  0.0 321.2 jit_solution(6578839213966138822)
XLA Ops:
  6.4 3.0 collective-permute-start.3
  11.0 2.6 collective-permute-start.1
  13.8 1.8 collective-permute-done
  15.6 7.4 %collective-permute-done.1 = bf16[160,384]{1,0:T(8,128)(2,1)S(1)} collective-permute-done((bf16[160,384]{1,0:T(8,128)(2,1)S(1)}, bf16[160,384]{1,0:T(8,128)(2,1)S(1)}, u32[]{:S(2)}, u32[]{:S(2)}) %collective-permute-start.1) | collective-permute-done | bytes 122912 | tf_op jit(solution)/shard_map/ppermute | solution.py:333
  26.8 2.9 collective-permute-start.6
  29.7 12.6 %collective-permute-done.7 = bf16[48,1536]{1,0:T(8,128)(2,1)S(1)} collective-permute-done((bf16[48,1536]{1,0:T(8,128)(2,1)S(1)}, bf16[48,1536]{1,0:T(8,128)(2,1)S(1)}, u32[]{:S(2)}, u32[]{:S(2)}) %collective-permute-start.7) | collective-permute-done | bytes 147488 | tf_op jit(solution)/shard_map/ppermute | solution.py:333
  42.4 2.7 collective-permute-start.13
  47.3 4.5 %collective-permute-done.13 = bf16[2,48,1920]{2,1,0:T(8,128)(2,1)S(1)} collective-permute-done((bf16[2,48,1920]{2,1,0:T(8,128)(2,1)S(1)}, bf16[2,48,1920]{2,1,0:T(8,128)(2,1)S(1)}, u32[]{:S(2)}, u32[]{:S(2)}) %collective-permute-start.13) | collective-permute-done | bytes 368672 | tf_op jit(solution)/shard_map/ppermute | solution.py:333
  60.1 3.7 %collective-permute-done.21 = bf16[2,48,1536]{2,1,0:T(8,128)(2,1)} collective-permute-done((bf16[2,48,1536]{2,1,0:T(8,128)(2,1)}, bf16[2,48,1536]{2,1,0:T(8,128)(2,1)}, u32[]{:S(2)}, u32[]{:S(2)}) %collective-permute-start.21) | collective-permute-done | bytes 294944 | tf_op jit(solution)/shard_map/ppermute | solution.py:333
  65.5 2.0 place.3
  68.3 1.9 copy-done.34
  70.2 1.8 lines.1
  72.0 5.2 %collective-permute-done.14.refs_1_ = bf16[4,48,1920]{2,1,0:T(8,128)(2,1)} collective-permute-done((bf16[4,48,1920]{2,1,0:T(8,128)(2,1)S(1)}, bf16[4,48,1920]{2,1,0:T(8,128)(2,1)}, u32[]{:S(2)}, u32[]{:S(2)}) %collective-permute-start.14) | collective-permute-done | bytes 737312 | tf_op jit(solution)/shard_map/ppermute | solution.py:333
  79.0 6.1 %add_convert_fusion.q_ref.k_ref.v_ref._c._l.earlier_ref = bf16[1024,2304]{1,0:T(8,128)(2,1)S(1)} fusion(bf16[1024,768]{1,0:T(8,128)(2,1)S(1)} %bitcast.151, bf16[768,2304]{1,0:T(8,128)(2,1)} %copy-done.34, f32[2304]{0:T(1024)S(1)} %reduce), kind=kOutput, calls=%fused_computation.2 | convolution fusion | flops 3628597248 | bytes 9839616 | tf_op jit(solution)/shard_map/dot_general | solution.py:31
  86.1 1.7 collective-permute-start.24
  87.8 8.2 %attend.2 = (bf16[1024,768]{1,0:T(8,128)(2,1)S(1)}, f32[1024,768]{1,0:T(8,128)S(1)}) custom-call(s32[3]{0:T(128)S(1)} %pad_add_fusion.info_ref, bf16[1024,2304]{1,0:T(8,128)(2,1)S(1)} %add_convert_fusion.q_ref.k_ref.v_ref._c._l.earlier_ref, bf16[1024,2304]{1,0:T(8,128)(2,1)S(1)} %add_convert_fusion.q_ref.k_ref.v_ref._c._l.earlier_ref, ...), custom_call_target="tpu_custom_call" | custom-call | flops 8999999488 | bytes 4718592 | tf_op jit(solution)/shard_map/attend/pallas_call | solution.py:86
  96.7 8.2 %attend.3 = (bf16[1024,768]{1,0:T(8,128)(2,1)S(1)}, f32[1024,768]{1,0:T(8,128)S(1)}) custom-call(s32[3]{0:T(128)S(1)} %pad_add_fusion.info_ref, bf16[1024,2304]{1,0:T(8,128)(2,1)S(1)} %add_convert_fusion.q_ref.k_ref.v_ref._c._l.earlier_ref, ...), custom_call_target="tpu_custom_call", output_to_operand_aliasing={{0}: (4, {}), {1}: (5, {})} | custom-call | flops 8999999488 | bytes 4718592 | tf_op jit(solution)/shard_map/attend/pallas_call | solution.py:86
  104.9 1.7 copy-done.39
  107.9 1.8 collective-permute-start.30
  109.7 2.1 place.4
  111.9 3.3 %attention_out.1 = (f32[1024,768]{1,0:T(8,128)S(1)}, bf16[1024,768]{1,0:T(8,128)(2,1)S(1)}, f32[1024,768]{1,0:T(8,128)S(1)}, f32[1024,128]{1,0:T(8,128)S(1)}) custom-call(bf16[1024,768]{1,0:T(8,128)(2,1)S(1)} %get-tuple-element.306.ctx_ref, bf16[768,768]{1,0:T(8,128)(2,1)S(1)} %get-tuple-element.315.w_ref, bf16[1024,768]{1,0:T(8,128)(2,1)S(1)} %bitcast.152, ...), custom_call_target="tpu_custom_call" | custom-call | flops 1207959552 | tf_op jit(solution)/shard_map/attention_out/pallas_call | solution.py:291
  116.2 8.0 %up.2 = (bf16[1024,3072]{1,0:T(8,128)(2,1)S(1)}, bf16[1024,3072]{1,0:T(8,128)(2,1)S(1)}) custom-call(bf16[1024,768]{1,0:T(8,128)(2,1)S(1)} %get-tuple-element.317.h_ref._g._s, bf16[768,3072]{1,0:T(8,128)(2,1)S(1)} %get-tuple-element.318.w_ref, f32[1,3072]{1,0:T(1,128)S(1)} %copy-done.16, bf16[1024,768]{1,0:T(8,128)(2,1)S(1)} %get-tuple-element.317.h_ref._g._s, ...), custom_call_target="tpu_custom_call" | custom-call | flops 8999999488 | bytes 6291456 | tf_op jit(solution)/shard_map/up/pallas_call | solution.py:216
  124.5 8.1 %up.3 = (bf16[1024,3072]{1,0:T(8,128)(2,1)S(1)}, bf16[1024,3072]{1,0:T(8,128)(2,1)S(1)}) custom-call(bf16[1024,768]{1,0:T(8,128)(2,1)S(1)} %get-tuple-element.317.h_ref._g._s, bf16[768,3072]{1,0:T(8,128)(2,1)S(1)} %get-tuple-element.318.w_ref, f32[1,3072]{1,0:T(1,128)S(1)} %copy-done.16, ...), custom_call_target="tpu_custom_call", output_to_operand_aliasing={{0}: (3, {}), {1}: (4, {})} | custom-call | flops 8999999488 | bytes 6291456 | tf_op jit(solution)/shard_map/up/pallas_call | solution.py:216
  135.4 1.8 copy-done.37
  137.2 2.8 copy-done.31
  140.0 9.2 %down.1 = (bf16[1024,768]{1,0:T(8,128)(2,1)S(1)}, f32[1024,768]{1,0:T(8,128)S(1)}, bf16[1024,768]{1,0:T(8,128)(2,1)}, f32[8,768]{1,0:T(8,128)S(1)}) custom-call(bf16[1024,3072]{1,0:T(8,128)(2,1)S(1)} %copy-done.31, bf16[768,3072]{1,0:T(8,128)(2,1)S(1)} %place.5.w_ref, f32[1024,768]{1,0:T(8,128)S(1)} %get-tuple-element.342.first_ref, ...), custom_call_target="tpu_custom_call" | custom-call | flops 4831838208 | tf_op jit(solution)/shard_map/down/pallas_call | solution.py:291
  150.7 6.8 %convolution_convert_fusion.1.refs_0_ = bf16[768,3072]{1,0:T(8,128)(2,1)S(1)} fusion(bf16[1024,768]{1,0:T(8,128)(2,1)} %get-tuple-element.358, bf16[1024,3072]{1,0:T(8,128)(2,1)S(1)} %copy-done.31), kind=kOutput, calls=%fused_computation.4 | convolution fusion | flops 4834197504 | bytes 12582912 | tf_op jit(solution)/shard_map/dot_general | solution.py:39
  158.9 1.8 collective-permute-start.33
  160.6 7.8 %multiply_convert_fusion.u_ref = bf16[1024,3072]{1,0:T(8,128)(2,1)S(1)} fusion(bf16[1024,3072]{1,0:T(8,128)(2,1)} %copy-done.37, bf16[1024,768]{1,0:T(8,128)(2,1)} %get-tuple-element.358, bf16[768,3072]{1,0:T(8,128)(2,1)S(1)} %place.5.w_ref), kind=kOutput, calls=%fused_computation.1 | convolution fusion | flops 4841275392 | bytes 18874368 | tf_op jit(solution)/shard_map/dot_general | solution.py:31
  169.9 5.4 %convolution_convert_fusion.refs_0_ = bf16[768,3072]{1,0:T(8,128)(2,1)S(1)} fusion(bf16[1024,768]{1,0:T(8,128)(2,1)S(1)} %copy-done.24, bf16[1024,3072]{1,0:T(8,128)(2,1)S(1)} %multiply_convert_fusion.u_ref), kind=kOutput, calls=%fused_computation.3 | convolution fusion | flops 4834197504 | bytes 12582912 | tf_op jit(solution)/shard_map/dot_general | solution.py:39
  177.0 1.8 fusion.11
  182.7 2.3 copy-done.18
  185.0 7.4 %up_back.1 = (f32[1024,768]{1,0:T(8,128)S(1)}, bf16[1024,768]{1,0:T(8,128)(2,1)S(1)}, f32[8,768]{1,0:T(8,128)S(1)}) custom-call(bf16[1024,3072]{1,0:T(8,128)(2,1)S(1)} %multiply_convert_fusion.u_ref, bf16[768,3072]{1,0:T(8,128)(2,1)S(1)} %copy-done.18, f32[1024,768]{1,0:T(8,128)S(1)} %get-tuple-element.372.second_ref, f32[1024,768]{1,0:T(8,128)S(1)} %copy-done.22, ...), custom_call_target="tpu_custom_call" | custom-call | flops 4831838208 | tf_op jit(solution)/shard_map/up_back/pallas_call | solution.py:291
  195.9 3.2 %collective-permute-done.37 = bf16[128,768]{1,0:T(8,128)(2,1)S(1)} collective-permute-done((bf16[128,768]{1,0:T(8,128)(2,1)S(1)}, bf16[128,768]{1,0:T(8,128)(2,1)S(1)}, u32[]{:S(2)}, u32[]{:S(2)}) %collective-permute-start.37) | collective-permute-done | bytes 196640 | tf_op jit(solution)/shard_map/ppermute | solution.py:611
  199.2 3.4 %fusion.15 = (bf16[4,48,1536]{2,1,0:T(8,128)(2,1)}, bf16[4,48,1536]{2,1,0:T(8,128)(2,1)S(1)}, bf16[4,48,1536]{2,1,0:T(8,128)(2,1)S(1)}, bf16[4,48,1536]{2,1,0:T(8,128)(2,1)}) fusion(bf16[4,4,48,1536]{3,2,1,0:T(8,128)(2,1)} %collective-permute-done.36, bf16[4,4,48,1536]{3,2,1,0:T(8,128)(2,1)S(1)} %get-tuple-element.383), kind=kLoop, calls=%fused_computation.53 | loop fusion | flops 4718592 | bytes 7077888 | tf_op jit(solution)/shard_map/convert_element_type | solution.py:547
  207.3 12.5 %attend_back.2 = (bf16[1024,2304]{1,0:T(8,128)(2,1)S(1)}, f32[8,2304]{1,0:T(8,128)S(1)}) custom-call(s32[3]{0:T(128)S(1)} %pad_add_fusion.info_ref, bf16[1024,2304]{1,0:T(8,128)(2,1)S(1)} %bitcast.157, bf16[1024,2304]{1,0:T(8,128)(2,1)S(1)} %bitcast.157, bf16[1024,2304]{1,0:T(8,128)(2,1)S(1)} %bitcast.157, bf16[1024,768]{1,0:T(8,128)(2,1)S(1)} %copy-done.27, ...), custom_call_target="tpu_custom_call" | custom-call | flops 16000000000 | bytes 5898240 | tf_op jit(solution)/shard_map/attend_back/pallas_call | solution.py:160
  221.0 2.0 slice_add_fusion.1
  232.0 12.9 %attend_back.3 = (bf16[1024,2304]{1,0:T(8,128)(2,1)S(1)}, f32[8,2304]{1,0:T(8,128)S(1)}) custom-call(s32[3]{0:T(128)S(1)} %pad_add_fusion.info_ref, bf16[1024,2304]{1,0:T(8,128)(2,1)S(1)} %bitcast.157, bf16[1024,2304]{1,0:T(8,128)(2,1)S(1)} %bitcast.157, bf16[1024,2304]{1,0:T(8,128)(2,1)S(1)} %bitcast.157, ...), custom_call_target="tpu_custom_call", output_to_operand_aliasing={{0}: (7, {})} | custom-call | flops 16000000000 | bytes 5898240 | tf_op jit(solution)/shard_map/attend_back/pallas_call | solution.py:160
  247.1 2.2 shares.1.refs_1_
  249.8 6.6 %convolution_convert_fusion.2.refs_0_ = bf16[768,2304]{1,0:T(8,128)(2,1)S(1)} fusion(bf16[1024,768]{1,0:T(8,128)(2,1)S(1)} %bitcast.153, bf16[1024,2304]{1,0:T(8,128)(2,1)} %copy-done.32), kind=kOutput, calls=%fused_computation.5 | convolution fusion | flops 3625648128 | bytes 9830400 | tf_op jit(solution)/shard_map/dot_general | solution.py:39
  258.0 1.9 add_convert_fusion.2
  261.6 2.0 slice_add_fusion
  267.0 2.9 collective-permute-done.48
  277.6 9.0 %collective-permute-done.51 = bf16[48,1536]{1,0:T(8,128)(2,1)} collective-permute-done((bf16[48,1536]{1,0:T(8,128)(2,1)}, bf16[48,1536]{1,0:T(8,128)(2,1)}, u32[]{:S(2)}, u32[]{:S(2)}) %collective-permute-start.51) | collective-permute-done | bytes 147488 | tf_op jit(solution)/shard_map/ppermute | solution.py:333
  299.5 4.1 %collective-permute-done.54 = bf16[4,160,384]{2,1,0:T(8,128)(2,1)S(1)} collective-permute-done((bf16[4,160,384]{2,1,0:T(8,128)(2,1)S(1)}, bf16[4,160,384]{2,1,0:T(8,128)(2,1)S(1)}, u32[]{:S(2)}, u32[]{:S(2)}) %collective-permute-start.54) | collective-permute-done | bytes 491552 | tf_op jit(solution)/shard_map/ppermute | solution.py:333
  309.3 2.2 collective-permute-start.59
  312.2 2.4 copy.41
  315.2 2.4 interleave.1
  (315 shorter events, 100.9 us)
Async XLA Ops:
  6.4 16.6 %collective-permute-start.3 = (bf16[1,256,768]{2,1,0:T(8,128)(2,1)S(1)}, bf16[1,256,768]{2,1,0:T(8,128)(2,1)S(1)}, u32[]{:S(2)}, u32[]{:S(2)}) collective-permute-start(bf16[1,256,768]{2,1,0:T(8,128)(2,1)S(1)} %slice.306), channel_id=1, source_target_pairs={{0,1},{1,0},{2,3},{3,2},{4,5},{5,4},{6,7},{7,6},{8,9},{9,8},{10,11... | collective-permute-start | bytes 1179656 | tf_op jit(solution)/shard_map/ppermute | solution.py:611
  11.0 12.0 %collective-permute-start.1 = (bf16[160,384]{1,0:T(8,128)(2,1)S(1)}, bf16[160,384]{1,0:T(8,128)(2,1)S(1)}, u32[]{:S(2)}, u32[]{:S(2)}) collective-permute-start(bf16[160,384]{1,0:T(8,128)(2,1)S(1)} %pad_maximum_fusion.8), channel_id=1, source_target_pairs={{0,16},{1,17},{2,18},{3,19},{4,20},{5,21},{6,22},{7,23},{8,24},{9,... | collective-permute-start | bytes 368648 | tf_op jit(solution)/shard_map/ppermute | solution.py:333
  13.6 9.4 %collective-permute-start.2 = (bf16[160,384]{1,0:T(8,128)(2,1)S(1)}, bf16[160,384]{1,0:T(8,128)(2,1)S(1)}, u32[]{:S(2)}, u32[]{:S(2)}) collective-permute-start(bf16[160,384]{1,0:T(8,128)(2,1)S(1)} %pad_maximum_fusion.8), channel_id=1, source_target_pairs={{0,24},{1,25},{2,26},{3,27},{4,28},{5,29},{6,30},{7,31},{8,16},{9,... | collective-permute-start | bytes 368648 | tf_op jit(solution)/shard_map/ppermute | solution.py:333
  23.1 19.3 %collective-permute-start.4 = (bf16[4,160,384]{2,1,0:T(8,128)(2,1)S(1)}, bf16[4,160,384]{2,1,0:T(8,128)(2,1)S(1)}, u32[]{:S(2)}, u32[]{:S(2)}) collective-permute-start(bf16[4,160,384]{2,1,0:T(8,128)(2,1)S(1)} %pad_maximum_fusion.4.refs_0_), channel_id=1, source_target_pairs={{0,4},{1,5},{2,3},{3,2},{4,0},{5,1},{6,7},{7,6},{8,12},{9,13},{10,... | collective-permute-start | bytes 1474568 | tf_op jit(solution)/shard_map/ppermute | solution.py:333
  24.6 17.7 %collective-permute-start.5 = (bf16[4,160,384]{2,1,0:T(8,128)(2,1)S(1)}, bf16[4,160,384]{2,1,0:T(8,128)(2,1)S(1)}, u32[]{:S(2)}, u32[]{:S(2)}) collective-permute-start(bf16[4,160,384]{2,1,0:T(8,128)(2,1)S(1)} %pad_maximum_fusion.4.refs_0_), channel_id=1, source_target_pairs={{0,1},{1,0},{2,6},{3,7},{4,5},{5,4},{6,2},{7,3},{8,9},{9,8},{10,14... | collective-permute-start | bytes 1474568 | tf_op jit(solution)/shard_map/ppermute | solution.py:333
  25.2 17.2 %collective-permute-start.8 = (bf16[1,256,768]{2,1,0:T(8,128)(2,1)S(1)}, bf16[1,256,768]{2,1,0:T(8,128)(2,1)S(1)}, u32[]{:S(2)}, u32[]{:S(2)}) collective-permute-start(bf16[1,256,768]{2,1,0:T(8,128)(2,1)S(1)} %slice.233), channel_id=1, source_target_pairs={{0,1},{1,0},{2,3},{3,2},{4,5},{5,4},{6,7},{7,6},{8,9},{9,8},{10,11... | collective-permute-start | bytes 1179656 | tf_op jit(solution)/shard_map/ppermute | solution.py:611
  26.8 15.6 %collective-permute-start.6 = (bf16[48,1920]{1,0:T(8,128)(2,1)S(1)}, bf16[48,1920]{1,0:T(8,128)(2,1)S(1)}, u32[]{:S(2)}, u32[]{:S(2)}) collective-permute-start(bf16[48,1920]{1,0:T(8,128)(2,1)S(1)} %pad_maximum_fusion.7), channel_id=1, source_target_pairs={{0,16},{1,17},{2,18},{3,19},{4,20},{5,21},{6,22},{7,23},{8,24},{9,... | collective-permute-start | bytes 552968 | tf_op jit(solution)/shard_map/ppermute | solution.py:333
  29.7 12.7 %collective-permute-start.7 = (bf16[48,1536]{1,0:T(8,128)(2,1)S(1)}, bf16[48,1536]{1,0:T(8,128)(2,1)S(1)}, u32[]{:S(2)}, u32[]{:S(2)}) collective-permute-start(bf16[48,1536]{1,0:T(8,128)(2,1)S(1)} %bitcast.167), channel_id=1, source_target_pairs={{0,16},{1,17},{2,18},{3,19},{4,20},{5,21},{6,22},{7,23},{8,24},{9,... | collective-permute-start | bytes 442376 | tf_op jit(solution)/shard_map/ppermute | solution.py:333
  42.4 9.4 %collective-permute-start.13 = (bf16[2,48,1920]{2,1,0:T(8,128)(2,1)S(1)}, bf16[2,48,1920]{2,1,0:T(8,128)(2,1)S(1)}, u32[]{:S(2)}, u32[]{:S(2)}) collective-permute-start(bf16[2,48,1920]{2,1,0:T(8,128)(2,1)S(1)} %pad_maximum_fusion.5), channel_id=1, source_target_pairs={{0,8},{1,9},{2,10},{3,11},{4,12},{5,13},{6,14},{7,15},{8,0},{9,1},... | collective-permute-start | bytes 1105928 | tf_op jit(solution)/shard_map/ppermute | solution.py:333
  45.3 9.7 %collective-permute-start.9 = (bf16[4,160,384]{2,1,0:T(8,128)(2,1)S(1)}, bf16[4,160,384]{2,1,0:T(8,128)(2,1)}, u32[]{:S(2)}, u32[]{:S(2)}) collective-permute-start(bf16[4,160,384]{2,1,0:T(8,128)(2,1)S(1)} %collective-permute-done.4.refs_1_), channel_id=1, source_target_pairs={{0,1},{1,0},{2,6},{3,7},{4,5},{5,4},{6,2},{7,3},{8,9},{9,8},{10,14... | collective-permute-start | bytes 1474568 | tf_op jit(solution)/shard_map/ppermute | solution.py:333
  58.1 19.2 %collective-permute-start.14 = (bf16[4,48,1920]{2,1,0:T(8,128)(2,1)S(1)}, bf16[4,48,1920]{2,1,0:T(8,128)(2,1)}, u32[]{:S(2)}, u32[]{:S(2)}) collective-permute-start(bf16[4,48,1920]{2,1,0:T(8,128)(2,1)S(1)} %pad_maximum_fusion.2.refs_0_), channel_id=1, source_target_pairs={{0,4},{1,5},{2,3},{3,2},{4,0},{5,1},{6,7},{7,6},{8,12},{9,13},{10,... | collective-permute-start | bytes 2211848 | tf_op jit(solution)/shard_map/ppermute | solution.py:333
  59.6 17.6 %collective-permute-start.15 = (bf16[4,48,1920]{2,1,0:T(8,128)(2,1)S(1)}, bf16[4,48,1920]{2,1,0:T(8,128)(2,1)}, u32[]{:S(2)}, u32[]{:S(2)}) collective-permute-start(bf16[4,48,1920]{2,1,0:T(8,128)(2,1)S(1)} %pad_maximum_fusion.2.refs_0_), channel_id=1, source_target_pairs={{0,1},{1,0},{2,6},{3,7},{4,5},{5,4},{6,2},{7,3},{8,9},{9,8},{10,14... | collective-permute-start | bytes 2211848 | tf_op jit(solution)/shard_map/ppermute | solution.py:333
  60.1 17.1 %collective-permute-start.16 = (bf16[4,48,1920]{2,1,0:T(8,128)(2,1)S(1)}, bf16[4,48,1920]{2,1,0:T(8,128)(2,1)}, u32[]{:S(2)}, u32[]{:S(2)}) collective-permute-start(bf16[4,48,1920]{2,1,0:T(8,128)(2,1)S(1)} %pad_maximum_fusion.2.refs_0_), channel_id=1, source_target_pairs={{0,2},{1,3},{2,0},{3,1},{4,6},{5,7},{6,4},{7,5},{8,10},{9,11},{10,... | collective-permute-start | bytes 2211848 | tf_op jit(solution)/shard_map/ppermute | solution.py:333
  77.2 18.8 %collective-permute-start.18 = (bf16[4,48,1920]{2,1,0:T(8,128)(2,1)}, bf16[4,48,1920]{2,1,0:T(8,128)(2,1)S(1)}, u32[]{:S(2)}, u32[]{:S(2)}) collective-permute-start(bf16[4,48,1920]{2,1,0:T(8,128)(2,1)} %collective-permute-done.14.refs_1_), channel_id=1, source_target_pairs={{0,1},{1,0},{2,6},{3,7},{4,5},{5,4},{6,2},{7,3},{8,9},{9,8},{10,14... | collective-permute-start | bytes 2211848 | tf_op jit(solution)/shard_map/ppermute | solution.py:333
  77.5 18.5 %collective-permute-start.19 = (bf16[4,48,1920]{2,1,0:T(8,128)(2,1)}, bf16[4,48,1920]{2,1,0:T(8,128)(2,1)}, u32[]{:S(2)}, u32[]{:S(2)}) collective-permute-start(bf16[4,48,1920]{2,1,0:T(8,128)(2,1)} %collective-permute-done.14.refs_1_), channel_id=1, source_target_pairs={{0,2},{1,3},{2,0},{3,1},{4,6},{5,7},{6,4},{7,5},{8,10},{9,11},{10,... | collective-permute-start | bytes 2211848 | tf_op jit(solution)/shard_map/ppermute | solution.py:333
  85.3 21.4 %collective-permute-start.23 = (bf16[4,48,1536]{2,1,0:T(8,128)(2,1)S(1)}, bf16[4,48,1536]{2,1,0:T(8,128)(2,1)S(1)}, u32[]{:S(2)}, u32[]{:S(2)}) collective-permute-start(bf16[4,48,1536]{2,1,0:T(8,128)(2,1)S(1)} %pad_maximum_fusion.3.refs_0_), channel_id=1, source_target_pairs={{0,4},{1,5},{2,3},{3,2},{4,0},{5,1},{6,7},{7,6},{8,12},{9,13},{10,... | collective-permute-start | bytes 1769480 | tf_op jit(solution)/shard_map/ppermute | solution.py:333
  86.1 20.6 %collective-permute-start.24 = (bf16[4,48,1536]{2,1,0:T(8,128)(2,1)S(1)}, bf16[4,48,1536]{2,1,0:T(8,128)(2,1)S(1)}, u32[]{:S(2)}, u32[]{:S(2)}) collective-permute-start(bf16[4,48,1536]{2,1,0:T(8,128)(2,1)S(1)} %pad_maximum_fusion.3.refs_0_), channel_id=1, source_target_pairs={{0,1},{1,0},{2,6},{3,7},{4,5},{5,4},{6,2},{7,3},{8,9},{9,8},{10,14... | collective-permute-start | bytes 1769480 | tf_op jit(solution)/shard_map/ppermute | solution.py:333
  96.1 10.6 %collective-permute-start.22 = (bf16[4,48,1920]{2,1,0:T(8,128)(2,1)S(1)}, bf16[4,48,1920]{2,1,0:T(8,128)(2,1)S(1)}, u32[]{:S(2)}, u32[]{:S(2)}) collective-permute-start(bf16[4,48,1920]{2,1,0:T(8,128)(2,1)S(1)} %collective-permute-done.18.refs_3_), channel_id=1, source_target_pairs={{0,2},{1,3},{2,0},{3,1},{4,6},{5,7},{6,4},{7,5},{8,10},{9,11},{10,... | collective-permute-start | bytes 2211848 | tf_op jit(solution)/shard_map/ppermute | solution.py:333
  106.7 17.5 %collective-permute-start.25 = (bf16[4,48,1536]{2,1,0:T(8,128)(2,1)S(1)}, bf16[4,48,1536]{2,1,0:T(8,128)(2,1)S(1)}, u32[]{:S(2)}, u32[]{:S(2)}) collective-permute-start(bf16[4,48,1536]{2,1,0:T(8,128)(2,1)S(1)} %collective-permute-done.23.refs_1_), channel_id=1, source_target_pairs={{0,1},{1,0},{2,6},{3,7},{4,5},{5,4},{6,2},{7,3},{8,9},{9,8},{10,14... | collective-permute-start | bytes 1769480 | tf_op jit(solution)/shard_map/ppermute | solution.py:333
  107.0 17.2 %collective-permute-start.27 = (bf16[4,48,1536]{2,1,0:T(8,128)(2,1)S(1)}, bf16[4,48,1536]{2,1,0:T(8,128)(2,1)S(1)}, u32[]{:S(2)}, u32[]{:S(2)}) collective-permute-start(bf16[4,48,1536]{2,1,0:T(8,128)(2,1)S(1)} %collective-permute-done.23.refs_1_), channel_id=1, source_target_pairs={{0,2},{1,3},{2,0},{3,1},{4,6},{5,7},{6,4},{7,5},{8,10},{9,11},{10,... | collective-permute-start | bytes 1769480 | tf_op jit(solution)/shard_map/ppermute | solution.py:333
  107.0 17.1 %collective-permute-start.26 = (bf16[4,48,1536]{2,1,0:T(8,128)(2,1)S(1)}, bf16[4,48,1536]{2,1,0:T(8,128)(2,1)S(1)}, u32[]{:S(2)}, u32[]{:S(2)}) collective-permute-start(bf16[4,48,1536]{2,1,0:T(8,128)(2,1)S(1)} %pad_maximum_fusion.3.refs_0_), channel_id=1, source_target_pairs={{0,2},{1,3},{2,0},{3,1},{4,6},{5,7},{6,4},{7,5},{8,10},{9,11},{10,... | collective-permute-start | bytes 1769480 | tf_op jit(solution)/shard_map/ppermute | solution.py:333
  107.6 16.7 %collective-permute-start.28 = (bf16[4,48,1536]{2,1,0:T(8,128)(2,1)S(1)}, bf16[4,48,1536]{2,1,0:T(8,128)(2,1)S(1)}, u32[]{:S(2)}, u32[]{:S(2)}) collective-permute-start(bf16[4,48,1536]{2,1,0:T(8,128)(2,1)S(1)} %collective-permute-done.24.refs_2_), channel_id=1, source_target_pairs={{0,2},{1,3},{2,0},{3,1},{4,6},{5,7},{6,4},{7,5},{8,10},{9,11},{10,... | collective-permute-start | bytes 1769480 | tf_op jit(solution)/shard_map/ppermute | solution.py:333
  107.9 25.6 %collective-permute-start.30 = (bf16[2,256,768]{2,1,0:T(8,128)(2,1)S(1)}, bf16[2,256,768]{2,1,0:T(8,128)(2,1)S(1)}, u32[]{:S(2)}, u32[]{:S(2)}) collective-permute-start(bf16[2,256,768]{2,1,0:T(8,128)(2,1)S(1)} %get-tuple-element.510), channel_id=1, source_target_pairs={{0,1},{1,0},{2,3},{3,2},{4,5},{5,4},{6,7},{7,6},{8,9},{9,8},{10,11... | collective-permute-start | bytes 2359304 | tf_op jit(solution)/shard_map/ppermute | solution.py:611
  158.8 9.7 %collective-permute-start.32 = (bf16[4,4,48,1536]{3,2,1,0:T(8,128)(2,1)S(1)}, bf16[4,4,48,1536]{3,2,1,0:T(8,128)(2,1)S(1)}, u32[]{:S(2)}, u32[]{:S(2)}) collective-permute-start(bf16[4,4,48,1536]{3,2,1,0:T(8,128)(2,1)S(1)} %get-tuple-element.357), channel_id=1, source_target_pairs={{0,2},{1,3},{2,0},{3,1},{4,6},{5,7},{6,4},{7,5},{8,10},{9,11},{10,... | collective-permute-start | bytes 7077896 | tf_op jit(solution)/shard_map/ppermute | solution.py:333
  158.9 9.6 %collective-permute-start.33 = (bf16[128,768]{1,0:T(8,128)(2,1)S(1)}, bf16[128,768]{1,0:T(8,128)(2,1)S(1)}, u32[]{:S(2)}, u32[]{:S(2)}) collective-permute-start(bf16[128,768]{1,0:T(8,128)(2,1)S(1)} %get-tuple-element.361), channel_id=1, source_target_pairs={{0,1},{1,0},{2,3},{3,2},{4,5},{5,4},{6,7},{7,6},{8,9},{9,8},{10,11... | collective-permute-start | bytes 589832 | tf_op jit(solution)/shard_map/ppermute | solution.py:611
  176.8 22.4 %collective-permute-start.36 = (bf16[4,4,48,1536]{3,2,1,0:T(8,128)(2,1)S(1)}, bf16[4,4,48,1536]{3,2,1,0:T(8,128)(2,1)}, u32[]{:S(2)}, u32[]{:S(2)}) collective-permute-start(bf16[4,4,48,1536]{3,2,1,0:T(8,128)(2,1)S(1)} %get-tuple-element.370), channel_id=1, source_target_pairs={{0,2},{1,3},{2,0},{3,1},{4,6},{5,7},{6,4},{7,5},{8,10},{9,11},{10,... | collective-permute-start | bytes 7077896 | tf_op jit(solution)/shard_map/ppermute | solution.py:333
  178.8 20.4 %collective-permute-start.34 = (bf16[4,48,1536]{2,1,0:T(8,128)(2,1)S(1)}, bf16[4,48,1536]{2,1,0:T(8,128)(2,1)}, u32[]{:S(2)}, u32[]{:S(2)}) collective-permute-start(bf16[4,48,1536]{2,1,0:T(8,128)(2,1)S(1)} %get-tuple-element.501), channel_id=1, source_target_pairs={{0,1},{1,0},{2,6},{3,7},{4,5},{5,4},{6,2},{7,3},{8,9},{9,8},{10,14... | collective-permute-start | bytes 1769480 | tf_op jit(solution)/shard_map/ppermute | solution.py:333
  179.1 20.1 %collective-permute-start.35 = (bf16[4,48,1536]{2,1,0:T(8,128)(2,1)S(1)}, bf16[4,48,1536]{2,1,0:T(8,128)(2,1)}, u32[]{:S(2)}, u32[]{:S(2)}) collective-permute-start(bf16[4,48,1536]{2,1,0:T(8,128)(2,1)S(1)} %get-tuple-element.500), channel_id=1, source_target_pairs={{0,1},{1,0},{2,6},{3,7},{4,5},{5,4},{6,2},{7,3},{8,9},{9,8},{10,14... | collective-permute-start | bytes 1769480 | tf_op jit(solution)/shard_map/ppermute | solution.py:333
  180.8 18.4 %collective-permute-start.37 = (bf16[128,768]{1,0:T(8,128)(2,1)S(1)}, bf16[128,768]{1,0:T(8,128)(2,1)S(1)}, u32[]{:S(2)}, u32[]{:S(2)}) collective-permute-start(bf16[128,768]{1,0:T(8,128)(2,1)S(1)} %get-tuple-element.378), channel_id=1, source_target_pairs={{0,1},{1,0},{2,3},{3,2},{4,5},{5,4},{6,7},{7,6},{8,9},{9,8},{10,11... | collective-permute-start | bytes 589832 | tf_op jit(solution)/shard_map/ppermute | solution.py:611
  202.7 17.1 %collective-permute-start.39 = (bf16[4,48,1536]{2,1,0:T(8,128)(2,1)S(1)}, bf16[4,48,1536]{2,1,0:T(8,128)(2,1)S(1)}, u32[]{:S(2)}, u32[]{:S(2)}) collective-permute-start(bf16[4,48,1536]{2,1,0:T(8,128)(2,1)S(1)} %get-tuple-element.497), channel_id=1, source_target_pairs={{0,1},{1,0},{2,6},{3,7},{4,5},{5,4},{6,2},{7,3},{8,9},{9,8},{10,14... | collective-permute-start | bytes 1769480 | tf_op jit(solution)/shard_map/ppermute | solution.py:333
  203.5 16.4 %collective-permute-start.40 = (bf16[4,4,48,384]{3,2,1,0:T(8,128)(2,1)S(1)}, bf16[4,4,48,384]{3,2,1,0:T(8,128)(2,1)S(1)}, u32[]{:S(2)}, u32[]{:S(2)}) collective-permute-start(bf16[4,4,48,384]{3,2,1,0:T(8,128)(2,1)S(1)} %get-tuple-element.387), channel_id=1, source_target_pairs={{0,2},{1,3},{2,0},{3,1},{4,6},{5,7},{6,4},{7,5},{8,10},{9,11},{10,... | collective-permute-start | bytes 1769480 | tf_op jit(solution)/shard_map/ppermute | solution.py:333
  205.3 15.7 %collective-permute-start.38 = (bf16[4,48,1536]{2,1,0:T(8,128)(2,1)S(1)}, bf16[4,48,1536]{2,1,0:T(8,128)(2,1)S(1)}, u32[]{:S(2)}, u32[]{:S(2)}) collective-permute-start(bf16[4,48,1536]{2,1,0:T(8,128)(2,1)S(1)} %add_convert_fusion.8), channel_id=1, source_target_pairs={{0,4},{1,5},{2,3},{3,2},{4,0},{5,1},{6,7},{7,6},{8,12},{9,13},{10,... | collective-permute-start | bytes 1769480 | tf_op jit(solution)/shard_map/ppermute | solution.py:333
  206.4 42.9 %collective-permute-start.42 = (bf16[4,48,1536]{2,1,0:T(8,128)(2,1)}, bf16[4,48,1536]{2,1,0:T(8,128)(2,1)}, u32[]{:S(2)}, u32[]{:S(2)}) collective-permute-start(bf16[4,48,1536]{2,1,0:T(8,128)(2,1)} %get-tuple-element.496), channel_id=1, source_target_pairs={{0,1},{1,0},{2,6},{3,7},{4,5},{5,4},{6,2},{7,3},{8,9},{9,8},{10,14... | collective-permute-start | bytes 1769480 | tf_op jit(solution)/shard_map/ppermute | solution.py:333
  223.9 25.9 %collective-permute-start.45 = (bf16[256,768]{1,0:T(8,128)(2,1)}, bf16[256,768]{1,0:T(8,128)(2,1)S(1)}, u32[]{:S(2)}, u32[]{:S(2)}) collective-permute-start(bf16[256,768]{1,0:T(8,128)(2,1)} %slice.416), channel_id=1, source_target_pairs={{0,1},{1,0},{2,3},{3,2},{4,5},{5,4},{6,7},{7,6},{8,9},{9,8},{10,11... | collective-permute-start | bytes 1179656 | tf_op jit(solution)/shard_map/ppermute | solution.py:611
  226.4 23.4 %collective-permute-start.43 = (bf16[4,48,384]{2,1,0:T(8,128)(2,1)}, bf16[4,48,384]{2,1,0:T(8,128)(2,1)}, u32[]{:S(2)}, u32[]{:S(2)}) collective-permute-start(bf16[4,48,384]{2,1,0:T(8,128)(2,1)} %get-tuple-element.515), channel_id=1, source_target_pairs={{0,1},{1,0},{2,6},{3,7},{4,5},{5,4},{6,2},{7,3},{8,9},{9,8},{10,14... | collective-permute-start | bytes 442376 | tf_op jit(solution)/shard_map/ppermute | solution.py:333
  226.8 22.9 %collective-permute-start.44 = (bf16[4,48,384]{2,1,0:T(8,128)(2,1)}, bf16[4,48,384]{2,1,0:T(8,128)(2,1)}, u32[]{:S(2)}, u32[]{:S(2)}) collective-permute-start(bf16[4,48,384]{2,1,0:T(8,128)(2,1)} %get-tuple-element.514), channel_id=1, source_target_pairs={{0,1},{1,0},{2,6},{3,7},{4,5},{5,4},{6,2},{7,3},{8,9},{9,8},{10,14... | collective-permute-start | bytes 442376 | tf_op jit(solution)/shard_map/ppermute | solution.py:333
  230.5 19.2 %collective-permute-start.41 = (bf16[2,48,1536]{2,1,0:T(8,128)(2,1)}, bf16[2,48,1536]{2,1,0:T(8,128)(2,1)}, u32[]{:S(2)}, u32[]{:S(2)}) collective-permute-start(bf16[2,48,1536]{2,1,0:T(8,128)(2,1)} %get-tuple-element.524), channel_id=1, source_target_pairs={{0,16},{1,17},{2,18},{3,19},{4,20},{5,21},{6,22},{7,23},{8,24},{9,... | collective-permute-start | bytes 884744 | tf_op jit(solution)/shard_map/ppermute | solution.py:333
  258.0 11.9 %collective-permute-start.47 = (bf16[4,4,160,384]{3,2,1,0:T(8,128)(2,1)S(1)}, bf16[4,4,160,384]{3,2,1,0:T(8,128)(2,1)S(1)}, u32[]{:S(2)}, u32[]{:S(2)}) collective-permute-start(bf16[4,4,160,384]{3,2,1,0:T(8,128)(2,1)S(1)} %get-tuple-element.418), channel_id=1, source_target_pairs={{0,2},{1,3},{2,0},{3,1},{4,6},{5,7},{6,4},{7,5},{8,10},{9,11},{10,... | collective-permute-start | bytes 5898248 | tf_op jit(solution)/shard_map/ppermute | solution.py:333
  259.9 9.9 %collective-permute-start.48 = (bf16[4,48,1536]{2,1,0:T(8,128)(2,1)S(1)}, bf16[4,48,1536]{2,1,0:T(8,128)(2,1)S(1)}, u32[]{:S(2)}, u32[]{:S(2)}) collective-permute-start(bf16[4,48,1536]{2,1,0:T(8,128)(2,1)S(1)} %add_convert_fusion.2), channel_id=1, source_target_pairs={{0,4},{1,5},{2,3},{3,2},{4,0},{5,1},{6,7},{7,6},{8,12},{9,13},{10,... | collective-permute-start | bytes 1769480 | tf_op jit(solution)/shard_map/ppermute | solution.py:333
  265.5 12.0 %collective-permute-start.53 = (bf16[4,48,384]{2,1,0:T(8,128)(2,1)S(1)}, bf16[4,48,384]{2,1,0:T(8,128)(2,1)}, u32[]{:S(2)}, u32[]{:S(2)}) collective-permute-start(bf16[4,48,384]{2,1,0:T(8,128)(2,1)S(1)} %add_convert_fusion.22), channel_id=1, source_target_pairs={{0,4},{1,5},{2,3},{3,2},{4,0},{5,1},{6,7},{7,6},{8,12},{9,13},{10,... | collective-permute-start | bytes 442376 | tf_op jit(solution)/shard_map/ppermute | solution.py:333
  270.9 15.7 %collective-permute-start.52 = (bf16[2,48,1536]{2,1,0:T(8,128)(2,1)}, bf16[2,48,1536]{2,1,0:T(8,128)(2,1)}, u32[]{:S(2)}, u32[]{:S(2)}) collective-permute-start(bf16[2,48,1536]{2,1,0:T(8,128)(2,1)} %get-tuple-element.522), channel_id=1, source_target_pairs={{0,16},{1,17},{2,18},{3,19},{4,20},{5,21},{6,22},{7,23},{8,24},{9,... | collective-permute-start | bytes 884744 | tf_op jit(solution)/shard_map/ppermute | solution.py:333
  273.8 12.8 %collective-permute-start.49 = (bf16[4,160,384]{2,1,0:T(8,128)(2,1)}, bf16[4,160,384]{2,1,0:T(8,128)(2,1)}, u32[]{:S(2)}, u32[]{:S(2)}) collective-permute-start(bf16[4,160,384]{2,1,0:T(8,128)(2,1)} %get-tuple-element.505), channel_id=1, source_target_pairs={{0,1},{1,0},{2,6},{3,7},{4,5},{5,4},{6,2},{7,3},{8,9},{9,8},{10,14... | collective-permute-start | bytes 1474568 | tf_op jit(solution)/shard_map/ppermute | solution.py:333
  275.3 12.8 %collective-permute-start.50 = (bf16[4,160,384]{2,1,0:T(8,128)(2,1)}, bf16[4,160,384]{2,1,0:T(8,128)(2,1)}, u32[]{:S(2)}, u32[]{:S(2)}) collective-permute-start(bf16[4,160,384]{2,1,0:T(8,128)(2,1)} %get-tuple-element.504), channel_id=1, source_target_pairs={{0,1},{1,0},{2,6},{3,7},{4,5},{5,4},{6,2},{7,3},{8,9},{9,8},{10,14... | collective-permute-start | bytes 1474568 | tf_op jit(solution)/shard_map/ppermute | solution.py:333
  276.5 10.0 %collective-permute-start.51 = (bf16[48,1536]{1,0:T(8,128)(2,1)}, bf16[48,1536]{1,0:T(8,128)(2,1)}, u32[]{:S(2)}, u32[]{:S(2)}) collective-permute-start(bf16[48,1536]{1,0:T(8,128)(2,1)} %get-tuple-element.534), channel_id=1, source_target_pairs={{0,8},{1,9},{2,10},{3,11},{4,12},{5,13},{6,14},{7,15},{8,0},{9,1},... | collective-permute-start | bytes 442376 | tf_op jit(solution)/shard_map/ppermute | solution.py:333
  289.3 10.2 %collective-permute-start.56 = (bf16[2,48,384]{2,1,0:T(8,128)(2,1)S(1)}, bf16[2,48,384]{2,1,0:T(8,128)(2,1)S(1)}, u32[]{:S(2)}, u32[]{:S(2)}) collective-permute-start(bf16[2,48,384]{2,1,0:T(8,128)(2,1)S(1)} %get-tuple-element.540), channel_id=1, source_target_pairs={{0,16},{1,17},{2,18},{3,19},{4,20},{5,21},{6,22},{7,23},{8,24},{9,... | collective-permute-start | bytes 221192 | tf_op jit(solution)/shard_map/ppermute | solution.py:333
  303.6 11.0 %collective-permute-start.61 = (bf16[48,384]{1,0:T(8,128)(2,1)S(1)}, bf16[48,384]{1,0:T(8,128)(2,1)S(1)}, u32[]{:S(2)}, u32[]{:S(2)}) collective-permute-start(bf16[48,384]{1,0:T(8,128)(2,1)S(1)} %slice_bitcast_fusion.17), channel_id=1, source_target_pairs={{0,8},{1,9},{2,10},{3,11},{4,12},{5,13},{6,14},{7,15},{8,0},{9,1},... | collective-permute-start | bytes 110600 | tf_op jit(solution)/shard_map/ppermute | solution.py:333
  304.2 11.1 %collective-permute-start.60 = (bf16[256,768]{1,0:T(8,128)(2,1)S(1)}, bf16[256,768]{1,0:T(8,128)(2,1)S(1)}, u32[]{:S(2)}, u32[]{:S(2)}) collective-permute-start(bf16[256,768]{1,0:T(8,128)(2,1)S(1)} %copy-done.58), channel_id=1, source_target_pairs={{0,1},{1,0},{2,3},{3,2},{4,5},{5,4},{6,7},{7,6},{8,9},{9,8},{10,11... | collective-permute-start | bytes 1179656 | tf_op jit(solution)/shard_map/ppermute | solution.py:611
  307.0 10.7 %collective-permute-start.57 = (bf16[160,384]{1,0:T(8,128)(2,1)S(1)}, bf16[160,384]{1,0:T(8,128)(2,1)S(1)}, u32[]{:S(2)}, u32[]{:S(2)}) collective-permute-start(bf16[160,384]{1,0:T(8,128)(2,1)S(1)} %get-tuple-element.528), channel_id=1, source_target_pairs={{0,8},{1,9},{2,10},{3,11},{4,12},{5,13},{6,14},{7,15},{8,0},{9,1},... | collective-permute-start | bytes 368648 | tf_op jit(solution)/shard_map/ppermute | solution.py:333
  (84 other events, 581.5 us)

commit v2 on v1

--- a/solution.py
+++ b/solution.py
@@ -837,14 +837,14 @@
         grad_vectors = pack(
             [shares(grad_pair, 2), shares(grad_in_bias, 1), shares(jnp.stack(grad_lines), 6)], bf16
         ).reshape(places * 16, local_width)
-    grad_wq, out_parts = sync(grad_wq, out_parts)
+    grad_wq, out_parts, into.held = sync(grad_wq, out_parts, into.held)
     triple = Reduce(
         me, [grad_wq, grad_vectors], qkv_moves, 3 * row + 16, local_width, direct
     )
     triple.held, grad_triple = sync(triple.held, grad_triple)
     triple.step()
     kept, sent = token_grads(seqs - 1)
-    triple.held, into.held, kept, sent = sync(triple.held, into.held, kept, sent)
+    triple.held, kept, sent = sync(triple.held, kept, sent)
     triple.step()
     into.step()
     down.step()

time: 325 us -> 325 us (level)
  waiting for transfers between devices: 58.1 us -> 61.5 us
    ppermute x53, waiting for transfers between devices: 54 us -> 57.4 us  [swap(): return lax.ppermute(value, BOTH, pairs)]
    unnamed x141 -> x151, local copies, waits for them, and re-layouts: 22.1 us -> 23.3 us
  transfers between devices with their start and end apart: 62 -> 62, of which waited for: 13 -> 16; matrix products, arithmetic and copies ran while one was open for 21% -> 20% of each run, Pallas kernels for 25% -> 26%
where the time goes in v2:
time: 325 us; the launch traced here: 322 us
  Pallas kernels  94 us (29%)
  waiting for transfers between devices  61.5 us (19%)
  starting transfers between devices  57 us (18%)
  matrix products  39.5 us (12%)
  local copies, waits for them, and re-layouts  38.6 us (12%)
  other arithmetic  28.9 us (9%)
    ppermute x53, waiting for transfers between devices, swap(): return lax.ppermute(value, BOTH, pairs)  57.4 us
    ppermute x53, starting transfers between devices, swap(): return lax.ppermute(value, BOTH, pairs)  45.3 us
    pallas_call x2, Pallas kernels, attend_back(): pl.pallas_call(functools.partial(attend_back_kernel, seq=seq), grid_spec=...  25.4 us
    unnamed x151, local copies, waits for them, and re-layouts  23.3 us
    dot_general x4, matrix products, dot_tn(): lax.dot_general(left, right, (((0,), (0,)), ((), ())), preferred_element_...  20.1 us
    pallas_call x3, Pallas kernels, by_rows(): pl.pallas_call(kernel, grid=(rows // step,), in_specs=[spec(value.shape,...  19.9 us
    convert_element_type x15, other arithmetic, add_low(): return sum((part.astype(f32) for part in parts)).astype(bf16)  19 us
    pallas_call x2, Pallas kernels, attend(): pl.pallas_call(functools.partial(attend_kernel, seq=seq), grid_spec=pltpu...  16.4 us
  transfers between devices with their start and end apart: 62, of which 16 were waited for; matrix products, arithmetic and copies ran while one was open for 20% of the time, Pallas kernels for 26%

profile of v2, /device:TPU:0, one launch (start us, length us, event | category | flops | bytes accessed | tf_op | source)
XLA Modules:
  0.0 321.6 jit_solution(12733130703918958295)
XLA Ops:
  6.4 3.0 collective-permute-start.3
  11.0 2.6 collective-permute-start.1
  13.8 1.8 collective-permute-done
  15.6 7.4 %collective-permute-done.1 = bf16[160,384]{1,0:T(8,128)(2,1)S(1)} collective-permute-done((bf16[160,384]{1,0:T(8,128)(2,1)S(1)}, bf16[160,384]{1,0:T(8,128)(2,1)S(1)}, u32[]{:S(2)}, u32[]{:S(2)}) %collective-permute-start.1) | collective-permute-done | bytes 122912 | tf_op jit(solution)/shard_map/ppermute | solution.py:333
  26.8 2.9 collective-permute-start.6
  29.7 12.6 %collective-permute-done.7 = bf16[48,1536]{1,0:T(8,128)(2,1)S(1)} collective-permute-done((bf16[48,1536]{1,0:T(8,128)(2,1)S(1)}, bf16[48,1536]{1,0:T(8,128)(2,1)S(1)}, u32[]{:S(2)}, u32[]{:S(2)}) %collective-permute-start.7) | collective-permute-done | bytes 147488 | tf_op jit(solution)/shard_map/ppermute | solution.py:333
  42.4 2.7 collective-permute-start.13
  47.3 4.5 %collective-permute-done.13 = bf16[2,48,1920]{2,1,0:T(8,128)(2,1)S(1)} collective-permute-done((bf16[2,48,1920]{2,1,0:T(8,128)(2,1)S(1)}, bf16[2,48,1920]{2,1,0:T(8,128)(2,1)S(1)}, u32[]{:S(2)}, u32[]{:S(2)}) %collective-permute-start.13) | collective-permute-done | bytes 368672 | tf_op jit(solution)/shard_map/ppermute | solution.py:333
  60.1 3.7 %collective-permute-done.21 = bf16[2,48,1536]{2,1,0:T(8,128)(2,1)} collective-permute-done((bf16[2,48,1536]{2,1,0:T(8,128)(2,1)}, bf16[2,48,1536]{2,1,0:T(8,128)(2,1)}, u32[]{:S(2)}, u32[]{:S(2)}) %collective-permute-start.21) | collective-permute-done | bytes 294944 | tf_op jit(solution)/shard_map/ppermute | solution.py:333
  65.5 2.0 place.3
  68.3 1.9 copy-done.33
  70.2 1.8 lines.1
  72.0 5.2 %collective-permute-done.14.refs_1_ = bf16[4,48,1920]{2,1,0:T(8,128)(2,1)} collective-permute-done((bf16[4,48,1920]{2,1,0:T(8,128)(2,1)S(1)}, bf16[4,48,1920]{2,1,0:T(8,128)(2,1)}, u32[]{:S(2)}, u32[]{:S(2)}) %collective-permute-start.14) | collective-permute-done | bytes 737312 | tf_op jit(solution)/shard_map/ppermute | solution.py:333
  79.0 6.1 %add_convert_fusion.q_ref.k_ref.v_ref._c._l.earlier_ref = bf16[1024,2304]{1,0:T(8,128)(2,1)S(1)} fusion(bf16[1024,768]{1,0:T(8,128)(2,1)S(1)} %bitcast.151, bf16[768,2304]{1,0:T(8,128)(2,1)} %copy-done.33, f32[2304]{0:T(1024)S(1)} %reduce), kind=kOutput, calls=%fused_computation.2 | convolution fusion | flops 3628597248 | bytes 9839616 | tf_op jit(solution)/shard_map/dot_general | solution.py:31
  86.1 1.7 collective-permute-start.24
  87.8 8.2 %attend.2 = (bf16[1024,768]{1,0:T(8,128)(2,1)S(1)}, f32[1024,768]{1,0:T(8,128)S(1)}) custom-call(s32[3]{0:T(128)S(1)} %pad_add_fusion.info_ref, bf16[1024,2304]{1,0:T(8,128)(2,1)S(1)} %add_convert_fusion.q_ref.k_ref.v_ref._c._l.earlier_ref, bf16[1024,2304]{1,0:T(8,128)(2,1)S(1)} %add_convert_fusion.q_ref.k_ref.v_ref._c._l.earlier_ref, ...), custom_call_target="tpu_custom_call" | custom-call | flops 8999999488 | bytes 4718592 | tf_op jit(solution)/shard_map/attend/pallas_call | solution.py:86
  96.7 8.2 %attend.3 = (bf16[1024,768]{1,0:T(8,128)(2,1)S(1)}, f32[1024,768]{1,0:T(8,128)S(1)}) custom-call(s32[3]{0:T(128)S(1)} %pad_add_fusion.info_ref, bf16[1024,2304]{1,0:T(8,128)(2,1)S(1)} %add_convert_fusion.q_ref.k_ref.v_ref._c._l.earlier_ref, ...), custom_call_target="tpu_custom_call", output_to_operand_aliasing={{0}: (4, {}), {1}: (5, {})} | custom-call | flops 8999999488 | bytes 4718592 | tf_op jit(solution)/shard_map/attend/pallas_call | solution.py:86
  107.9 1.8 collective-permute-start.30
  109.7 2.1 place.4
  111.8 3.3 %attention_out.1 = (f32[1024,768]{1,0:T(8,128)S(1)}, bf16[1024,768]{1,0:T(8,128)(2,1)S(1)}, f32[1024,768]{1,0:T(8,128)S(1)}, f32[1024,128]{1,0:T(8,128)S(1)}) custom-call(bf16[1024,768]{1,0:T(8,128)(2,1)S(1)} %get-tuple-element.306.ctx_ref, bf16[768,768]{1,0:T(8,128)(2,1)S(1)} %get-tuple-element.315.w_ref, bf16[1024,768]{1,0:T(8,128)(2,1)S(1)} %bitcast.152, ...), custom_call_target="tpu_custom_call" | custom-call | flops 1207959552 | tf_op jit(solution)/shard_map/attention_out/pallas_call | solution.py:291
  116.2 8.0 %up.2 = (bf16[1024,3072]{1,0:T(8,128)(2,1)S(1)}, bf16[1024,3072]{1,0:T(8,128)(2,1)S(1)}) custom-call(bf16[1024,768]{1,0:T(8,128)(2,1)S(1)} %get-tuple-element.317.h_ref._g._s, bf16[768,3072]{1,0:T(8,128)(2,1)S(1)} %get-tuple-element.318.w_ref, f32[1,3072]{1,0:T(1,128)S(1)} %copy-done.16, bf16[1024,768]{1,0:T(8,128)(2,1)S(1)} %get-tuple-element.317.h_ref._g._s, ...), custom_call_target="tpu_custom_call" | custom-call | flops 8999999488 | bytes 6291456 | tf_op jit(solution)/shard_map/up/pallas_call | solution.py:216
  124.5 8.1 %up.3 = (bf16[1024,3072]{1,0:T(8,128)(2,1)S(1)}, bf16[1024,3072]{1,0:T(8,128)(2,1)S(1)}) custom-call(bf16[1024,768]{1,0:T(8,128)(2,1)S(1)} %get-tuple-element.317.h_ref._g._s, bf16[768,3072]{1,0:T(8,128)(2,1)S(1)} %get-tuple-element.318.w_ref, f32[1,3072]{1,0:T(1,128)S(1)} %copy-done.16, ...), custom_call_target="tpu_custom_call", output_to_operand_aliasing={{0}: (3, {}), {1}: (4, {})} | custom-call | flops 8999999488 | bytes 6291456 | tf_op jit(solution)/shard_map/up/pallas_call | solution.py:216
  135.3 1.8 copy-done.36
  137.2 2.8 copy-done.31
  140.0 9.2 %down.1 = (bf16[1024,768]{1,0:T(8,128)(2,1)S(1)}, f32[1024,768]{1,0:T(8,128)S(1)}, bf16[1024,768]{1,0:T(8,128)(2,1)}, f32[8,768]{1,0:T(8,128)S(1)}) custom-call(bf16[1024,3072]{1,0:T(8,128)(2,1)S(1)} %copy-done.31, bf16[768,3072]{1,0:T(8,128)(2,1)S(1)} %place.5.w_ref, f32[1024,768]{1,0:T(8,128)S(1)} %get-tuple-element.342.first_ref, ...), custom_call_target="tpu_custom_call" | custom-call | flops 4831838208 | tf_op jit(solution)/shard_map/down/pallas_call | solution.py:291
  150.7 6.8 %convolution_convert_fusion.1.refs_0_ = bf16[768,3072]{1,0:T(8,128)(2,1)S(1)} fusion(bf16[1024,768]{1,0:T(8,128)(2,1)} %get-tuple-element.358, bf16[1024,3072]{1,0:T(8,128)(2,1)S(1)} %copy-done.31), kind=kOutput, calls=%fused_computation.4 | convolution fusion | flops 4834197504 | bytes 12582912 | tf_op jit(solution)/shard_map/dot_general | solution.py:39
  158.9 1.8 collective-permute-start.33
  160.6 7.8 %multiply_convert_fusion.u_ref = bf16[1024,3072]{1,0:T(8,128)(2,1)S(1)} fusion(bf16[1024,3072]{1,0:T(8,128)(2,1)} %copy-done.36, bf16[1024,768]{1,0:T(8,128)(2,1)} %get-tuple-element.358, bf16[768,3072]{1,0:T(8,128)(2,1)S(1)} %place.5.w_ref), kind=kOutput, calls=%fused_computation.1 | convolution fusion | flops 4841275392 | bytes 18874368 | tf_op jit(solution)/shard_map/dot_general | solution.py:31
  169.9 5.4 %convolution_convert_fusion.refs_0_ = bf16[768,3072]{1,0:T(8,128)(2,1)S(1)} fusion(bf16[1024,768]{1,0:T(8,128)(2,1)S(1)} %copy-done.24, bf16[1024,3072]{1,0:T(8,128)(2,1)S(1)} %multiply_convert_fusion.u_ref), kind=kOutput, calls=%fused_computation.3 | convolution fusion | flops 4834197504 | bytes 12582912 | tf_op jit(solution)/shard_map/dot_general | solution.py:39
  177.0 1.8 fusion.11
  182.7 2.3 copy-done.18
  185.0 7.4 %up_back.1 = (f32[1024,768]{1,0:T(8,128)S(1)}, bf16[1024,768]{1,0:T(8,128)(2,1)S(1)}, f32[8,768]{1,0:T(8,128)S(1)}) custom-call(bf16[1024,3072]{1,0:T(8,128)(2,1)S(1)} %multiply_convert_fusion.u_ref, bf16[768,3072]{1,0:T(8,128)(2,1)S(1)} %copy-done.18, f32[1024,768]{1,0:T(8,128)S(1)} %get-tuple-element.372.second_ref, f32[1024,768]{1,0:T(8,128)S(1)} %copy-done.22, ...), custom_call_target="tpu_custom_call" | custom-call | flops 4831838208 | tf_op jit(solution)/shard_map/up_back/pallas_call | solution.py:291
  196.0 3.3 %collective-permute-done.37 = bf16[128,768]{1,0:T(8,128)(2,1)S(1)} collective-permute-done((bf16[128,768]{1,0:T(8,128)(2,1)S(1)}, bf16[128,768]{1,0:T(8,128)(2,1)S(1)}, u32[]{:S(2)}, u32[]{:S(2)}) %collective-permute-start.37) | collective-permute-done | bytes 196640 | tf_op jit(solution)/shard_map/ppermute | solution.py:611
  199.3 3.4 %fusion.15 = (bf16[4,48,1536]{2,1,0:T(8,128)(2,1)}, bf16[4,48,1536]{2,1,0:T(8,128)(2,1)S(1)}, bf16[4,48,1536]{2,1,0:T(8,128)(2,1)S(1)}, bf16[4,48,1536]{2,1,0:T(8,128)(2,1)}) fusion(bf16[4,4,48,1536]{3,2,1,0:T(8,128)(2,1)} %collective-permute-done.36, bf16[4,4,48,1536]{3,2,1,0:T(8,128)(2,1)S(1)} %get-tuple-element.383), kind=kLoop, calls=%fused_computation.53 | loop fusion | flops 4718592 | bytes 7077888 | tf_op jit(solution)/shard_map/convert_element_type | solution.py:547
  207.4 12.5 %attend_back.2 = (bf16[1024,2304]{1,0:T(8,128)(2,1)S(1)}, f32[8,2304]{1,0:T(8,128)S(1)}) custom-call(s32[3]{0:T(128)S(1)} %pad_add_fusion.info_ref, bf16[1024,2304]{1,0:T(8,128)(2,1)S(1)} %bitcast.159, bf16[1024,2304]{1,0:T(8,128)(2,1)S(1)} %bitcast.159, bf16[1024,2304]{1,0:T(8,128)(2,1)S(1)} %bitcast.159, bf16[1024,768]{1,0:T(8,128)(2,1)S(1)} %copy-done.27, ...), custom_call_target="tpu_custom_call" | custom-call | flops 16000000000 | bytes 5898240 | tf_op jit(solution)/shard_map/attend_back/pallas_call | solution.py:160
  221.0 2.0 slice_add_fusion.1
  232.0 12.9 %attend_back.3 = (bf16[1024,2304]{1,0:T(8,128)(2,1)S(1)}, f32[8,2304]{1,0:T(8,128)S(1)}) custom-call(s32[3]{0:T(128)S(1)} %pad_add_fusion.info_ref, bf16[1024,2304]{1,0:T(8,128)(2,1)S(1)} %bitcast.159, bf16[1024,2304]{1,0:T(8,128)(2,1)S(1)} %bitcast.159, bf16[1024,2304]{1,0:T(8,128)(2,1)S(1)} %bitcast.159, ...), custom_call_target="tpu_custom_call", output_to_operand_aliasing={{0}: (7, {})} | custom-call | flops 16000000000 | bytes 5898240 | tf_op jit(solution)/shard_map/attend_back/pallas_call | solution.py:160
  247.1 2.2 shares.1.refs_1_
  254.8 6.4 %convolution_convert_fusion.2.refs_0_ = bf16[768,2304]{1,0:T(8,128)(2,1)S(1)} fusion(bf16[1024,768]{1,0:T(8,128)(2,1)S(1)} %bitcast.153, bf16[1024,2304]{1,0:T(8,128)(2,1)} %copy-done.32), kind=kOutput, calls=%fused_computation.5 | convolution fusion | flops 3625648128 | bytes 9830400 | tf_op jit(solution)/shard_map/dot_general | solution.py:39
  262.0 2.2 collective-permute-done.47
  266.9 2.0 slice_add_fusion
  277.1 6.1 %collective-permute-done.51 = bf16[48,1536]{1,0:T(8,128)(2,1)S(1)} collective-permute-done((bf16[48,1536]{1,0:T(8,128)(2,1)}, bf16[48,1536]{1,0:T(8,128)(2,1)S(1)}, u32[]{:S(2)}, u32[]{:S(2)}) %collective-permute-start.51) | collective-permute-done | bytes 147488 | tf_op jit(solution)/shard_map/ppermute | solution.py:333
  283.2 5.0 %collective-permute-done.52 = bf16[2,48,1536]{2,1,0:T(8,128)(2,1)} collective-permute-done((bf16[2,48,1536]{2,1,0:T(8,128)(2,1)}, bf16[2,48,1536]{2,1,0:T(8,128)(2,1)}, u32[]{:S(2)}, u32[]{:S(2)}) %collective-permute-start.52) | collective-permute-done | bytes 294944 | tf_op jit(solution)/shard_map/ppermute | solution.py:333
  298.1 5.9 %collective-permute-done.54 = bf16[4,160,384]{2,1,0:T(8,128)(2,1)S(1)} collective-permute-done((bf16[4,160,384]{2,1,0:T(8,128)(2,1)S(1)}, bf16[4,160,384]{2,1,0:T(8,128)(2,1)S(1)}, u32[]{:S(2)}, u32[]{:S(2)}) %collective-permute-start.54) | collective-permute-done | bytes 491552 | tf_op jit(solution)/shard_map/ppermute | solution.py:333
  306.7 2.0 collective-permute-start.57
  309.2 2.0 collective-permute-start.59
  311.9 2.4 copy.41
  314.9 2.4 interleave.1
  (326 shorter events, 99.9 us)
Async XLA Ops:
  6.4 16.6 %collective-permute-start.3 = (bf16[1,256,768]{2,1,0:T(8,128)(2,1)S(1)}, bf16[1,256,768]{2,1,0:T(8,128)(2,1)S(1)}, u32[]{:S(2)}, u32[]{:S(2)}) collective-permute-start(bf16[1,256,768]{2,1,0:T(8,128)(2,1)S(1)} %slice.306), channel_id=1, source_target_pairs={{0,1},{1,0},{2,3},{3,2},{4,5},{5,4},{6,7},{7,6},{8,9},{9,8},{10,11... | collective-permute-start | bytes 1179656 | tf_op jit(solution)/shard_map/ppermute | solution.py:611
  11.0 12.0 %collective-permute-start.1 = (bf16[160,384]{1,0:T(8,128)(2,1)S(1)}, bf16[160,384]{1,0:T(8,128)(2,1)S(1)}, u32[]{:S(2)}, u32[]{:S(2)}) collective-permute-start(bf16[160,384]{1,0:T(8,128)(2,1)S(1)} %pad_maximum_fusion.8), channel_id=1, source_target_pairs={{0,16},{1,17},{2,18},{3,19},{4,20},{5,21},{6,22},{7,23},{8,24},{9,... | collective-permute-start | bytes 368648 | tf_op jit(solution)/shard_map/ppermute | solution.py:333
  13.6 9.4 %collective-permute-start.2 = (bf16[160,384]{1,0:T(8,128)(2,1)S(1)}, bf16[160,384]{1,0:T(8,128)(2,1)S(1)}, u32[]{:S(2)}, u32[]{:S(2)}) collective-permute-start(bf16[160,384]{1,0:T(8,128)(2,1)S(1)} %pad_maximum_fusion.8), channel_id=1, source_target_pairs={{0,24},{1,25},{2,26},{3,27},{4,28},{5,29},{6,30},{7,31},{8,16},{9,... | collective-permute-start | bytes 368648 | tf_op jit(solution)/shard_map/ppermute | solution.py:333
  23.1 19.3 %collective-permute-start.4 = (bf16[4,160,384]{2,1,0:T(8,128)(2,1)S(1)}, bf16[4,160,384]{2,1,0:T(8,128)(2,1)S(1)}, u32[]{:S(2)}, u32[]{:S(2)}) collective-permute-start(bf16[4,160,384]{2,1,0:T(8,128)(2,1)S(1)} %pad_maximum_fusion.4.refs_0_), channel_id=1, source_target_pairs={{0,4},{1,5},{2,3},{3,2},{4,0},{5,1},{6,7},{7,6},{8,12},{9,13},{10,... | collective-permute-start | bytes 1474568 | tf_op jit(solution)/shard_map/ppermute | solution.py:333
  24.6 17.7 %collective-permute-start.5 = (bf16[4,160,384]{2,1,0:T(8,128)(2,1)S(1)}, bf16[4,160,384]{2,1,0:T(8,128)(2,1)S(1)}, u32[]{:S(2)}, u32[]{:S(2)}) collective-permute-start(bf16[4,160,384]{2,1,0:T(8,128)(2,1)S(1)} %pad_maximum_fusion.4.refs_0_), channel_id=1, source_target_pairs={{0,1},{1,0},{2,6},{3,7},{4,5},{5,4},{6,2},{7,3},{8,9},{9,8},{10,14... | collective-permute-start | bytes 1474568 | tf_op jit(solution)/shard_map/ppermute | solution.py:333
  25.2 17.2 %collective-permute-start.8 = (bf16[1,256,768]{2,1,0:T(8,128)(2,1)S(1)}, bf16[1,256,768]{2,1,0:T(8,128)(2,1)S(1)}, u32[]{:S(2)}, u32[]{:S(2)}) collective-permute-start(bf16[1,256,768]{2,1,0:T(8,128)(2,1)S(1)} %slice.233), channel_id=1, source_target_pairs={{0,1},{1,0},{2,3},{3,2},{4,5},{5,4},{6,7},{7,6},{8,9},{9,8},{10,11... | collective-permute-start | bytes 1179656 | tf_op jit(solution)/shard_map/ppermute | solution.py:611
  26.8 15.6 %collective-permute-start.6 = (bf16[48,1920]{1,0:T(8,128)(2,1)S(1)}, bf16[48,1920]{1,0:T(8,128)(2,1)S(1)}, u32[]{:S(2)}, u32[]{:S(2)}) collective-permute-start(bf16[48,1920]{1,0:T(8,128)(2,1)S(1)} %pad_maximum_fusion.7), channel_id=1, source_target_pairs={{0,16},{1,17},{2,18},{3,19},{4,20},{5,21},{6,22},{7,23},{8,24},{9,... | collective-permute-start | bytes 552968 | tf_op jit(solution)/shard_map/ppermute | solution.py:333
  29.7 12.7 %collective-permute-start.7 = (bf16[48,1536]{1,0:T(8,128)(2,1)S(1)}, bf16[48,1536]{1,0:T(8,128)(2,1)S(1)}, u32[]{:S(2)}, u32[]{:S(2)}) collective-permute-start(bf16[48,1536]{1,0:T(8,128)(2,1)S(1)} %bitcast.169), channel_id=1, source_target_pairs={{0,16},{1,17},{2,18},{3,19},{4,20},{5,21},{6,22},{7,23},{8,24},{9,... | collective-permute-start | bytes 442376 | tf_op jit(solution)/shard_map/ppermute | solution.py:333
  42.4 9.4 %collective-permute-start.13 = (bf16[2,48,1920]{2,1,0:T(8,128)(2,1)S(1)}, bf16[2,48,1920]{2,1,0:T(8,128)(2,1)S(1)}, u32[]{:S(2)}, u32[]{:S(2)}) collective-permute-start(bf16[2,48,1920]{2,1,0:T(8,128)(2,1)S(1)} %pad_maximum_fusion.5), channel_id=1, source_target_pairs={{0,8},{1,9},{2,10},{3,11},{4,12},{5,13},{6,14},{7,15},{8,0},{9,1},... | collective-permute-start | bytes 1105928 | tf_op jit(solution)/shard_map/ppermute | solution.py:333
  45.3 9.7 %collective-permute-start.9 = (bf16[4,160,384]{2,1,0:T(8,128)(2,1)S(1)}, bf16[4,160,384]{2,1,0:T(8,128)(2,1)}, u32[]{:S(2)}, u32[]{:S(2)}) collective-permute-start(bf16[4,160,384]{2,1,0:T(8,128)(2,1)S(1)} %collective-permute-done.4.refs_1_), channel_id=1, source_target_pairs={{0,1},{1,0},{2,6},{3,7},{4,5},{5,4},{6,2},{7,3},{8,9},{9,8},{10,14... | collective-permute-start | bytes 1474568 | tf_op jit(solution)/shard_map/ppermute | solution.py:333
  58.1 19.2 %collective-permute-start.14 = (bf16[4,48,1920]{2,1,0:T(8,128)(2,1)S(1)}, bf16[4,48,1920]{2,1,0:T(8,128)(2,1)}, u32[]{:S(2)}, u32[]{:S(2)}) collective-permute-start(bf16[4,48,1920]{2,1,0:T(8,128)(2,1)S(1)} %pad_maximum_fusion.2.refs_0_), channel_id=1, source_target_pairs={{0,4},{1,5},{2,3},{3,2},{4,0},{5,1},{6,7},{7,6},{8,12},{9,13},{10,... | collective-permute-start | bytes 2211848 | tf_op jit(solution)/shard_map/ppermute | solution.py:333
  59.6 17.6 %collective-permute-start.15 = (bf16[4,48,1920]{2,1,0:T(8,128)(2,1)S(1)}, bf16[4,48,1920]{2,1,0:T(8,128)(2,1)}, u32[]{:S(2)}, u32[]{:S(2)}) collective-permute-start(bf16[4,48,1920]{2,1,0:T(8,128)(2,1)S(1)} %pad_maximum_fusion.2.refs_0_), channel_id=1, source_target_pairs={{0,1},{1,0},{2,6},{3,7},{4,5},{5,4},{6,2},{7,3},{8,9},{9,8},{10,14... | collective-permute-start | bytes 2211848 | tf_op jit(solution)/shard_map/ppermute | solution.py:333
  60.1 17.1 %collective-permute-start.16 = (bf16[4,48,1920]{2,1,0:T(8,128)(2,1)S(1)}, bf16[4,48,1920]{2,1,0:T(8,128)(2,1)}, u32[]{:S(2)}, u32[]{:S(2)}) collective-permute-start(bf16[4,48,1920]{2,1,0:T(8,128)(2,1)S(1)} %pad_maximum_fusion.2.refs_0_), channel_id=1, source_target_pairs={{0,2},{1,3},{2,0},{3,1},{4,6},{5,7},{6,4},{7,5},{8,10},{9,11},{10,... | collective-permute-start | bytes 2211848 | tf_op jit(solution)/shard_map/ppermute | solution.py:333
  77.2 18.8 %collective-permute-start.18 = (bf16[4,48,1920]{2,1,0:T(8,128)(2,1)}, bf16[4,48,1920]{2,1,0:T(8,128)(2,1)S(1)}, u32[]{:S(2)}, u32[]{:S(2)}) collective-permute-start(bf16[4,48,1920]{2,1,0:T(8,128)(2,1)} %collective-permute-done.14.refs_1_), channel_id=1, source_target_pairs={{0,1},{1,0},{2,6},{3,7},{4,5},{5,4},{6,2},{7,3},{8,9},{9,8},{10,14... | collective-permute-start | bytes 2211848 | tf_op jit(solution)/shard_map/ppermute | solution.py:333
  77.5 18.6 %collective-permute-start.19 = (bf16[4,48,1920]{2,1,0:T(8,128)(2,1)}, bf16[4,48,1920]{2,1,0:T(8,128)(2,1)}, u32[]{:S(2)}, u32[]{:S(2)}) collective-permute-start(bf16[4,48,1920]{2,1,0:T(8,128)(2,1)} %collective-permute-done.14.refs_1_), channel_id=1, source_target_pairs={{0,2},{1,3},{2,0},{3,1},{4,6},{5,7},{6,4},{7,5},{8,10},{9,11},{10,... | collective-permute-start | bytes 2211848 | tf_op jit(solution)/shard_map/ppermute | solution.py:333
  85.3 21.4 %collective-permute-start.23 = (bf16[4,48,1536]{2,1,0:T(8,128)(2,1)S(1)}, bf16[4,48,1536]{2,1,0:T(8,128)(2,1)S(1)}, u32[]{:S(2)}, u32[]{:S(2)}) collective-permute-start(bf16[4,48,1536]{2,1,0:T(8,128)(2,1)S(1)} %pad_maximum_fusion.3.refs_0_), channel_id=1, source_target_pairs={{0,4},{1,5},{2,3},{3,2},{4,0},{5,1},{6,7},{7,6},{8,12},{9,13},{10,... | collective-permute-start | bytes 1769480 | tf_op jit(solution)/shard_map/ppermute | solution.py:333
  86.1 20.5 %collective-permute-start.24 = (bf16[4,48,1536]{2,1,0:T(8,128)(2,1)S(1)}, bf16[4,48,1536]{2,1,0:T(8,128)(2,1)S(1)}, u32[]{:S(2)}, u32[]{:S(2)}) collective-permute-start(bf16[4,48,1536]{2,1,0:T(8,128)(2,1)S(1)} %pad_maximum_fusion.3.refs_0_), channel_id=1, source_target_pairs={{0,1},{1,0},{2,6},{3,7},{4,5},{5,4},{6,2},{7,3},{8,9},{9,8},{10,14... | collective-permute-start | bytes 1769480 | tf_op jit(solution)/shard_map/ppermute | solution.py:333
  96.1 10.5 %collective-permute-start.22 = (bf16[4,48,1920]{2,1,0:T(8,128)(2,1)S(1)}, bf16[4,48,1920]{2,1,0:T(8,128)(2,1)S(1)}, u32[]{:S(2)}, u32[]{:S(2)}) collective-permute-start(bf16[4,48,1920]{2,1,0:T(8,128)(2,1)S(1)} %collective-permute-done.18.refs_3_), channel_id=1, source_target_pairs={{0,2},{1,3},{2,0},{3,1},{4,6},{5,7},{6,4},{7,5},{8,10},{9,11},{10,... | collective-permute-start | bytes 2211848 | tf_op jit(solution)/shard_map/ppermute | solution.py:333
  106.7 17.5 %collective-permute-start.25 = (bf16[4,48,1536]{2,1,0:T(8,128)(2,1)S(1)}, bf16[4,48,1536]{2,1,0:T(8,128)(2,1)S(1)}, u32[]{:S(2)}, u32[]{:S(2)}) collective-permute-start(bf16[4,48,1536]{2,1,0:T(8,128)(2,1)S(1)} %collective-permute-done.23.refs_1_), channel_id=1, source_target_pairs={{0,1},{1,0},{2,6},{3,7},{4,5},{5,4},{6,2},{7,3},{8,9},{9,8},{10,14... | collective-permute-start | bytes 1769480 | tf_op jit(solution)/shard_map/ppermute | solution.py:333
  107.0 17.2 %collective-permute-start.27 = (bf16[4,48,1536]{2,1,0:T(8,128)(2,1)S(1)}, bf16[4,48,1536]{2,1,0:T(8,128)(2,1)S(1)}, u32[]{:S(2)}, u32[]{:S(2)}) collective-permute-start(bf16[4,48,1536]{2,1,0:T(8,128)(2,1)S(1)} %collective-permute-done.23.refs_1_), channel_id=1, source_target_pairs={{0,2},{1,3},{2,0},{3,1},{4,6},{5,7},{6,4},{7,5},{8,10},{9,11},{10,... | collective-permute-start | bytes 1769480 | tf_op jit(solution)/shard_map/ppermute | solution.py:333
  107.0 17.2 %collective-permute-start.26 = (bf16[4,48,1536]{2,1,0:T(8,128)(2,1)S(1)}, bf16[4,48,1536]{2,1,0:T(8,128)(2,1)S(1)}, u32[]{:S(2)}, u32[]{:S(2)}) collective-permute-start(bf16[4,48,1536]{2,1,0:T(8,128)(2,1)S(1)} %pad_maximum_fusion.3.refs_0_), channel_id=1, source_target_pairs={{0,2},{1,3},{2,0},{3,1},{4,6},{5,7},{6,4},{7,5},{8,10},{9,11},{10,... | collective-permute-start | bytes 1769480 | tf_op jit(solution)/shard_map/ppermute | solution.py:333
  107.5 16.7 %collective-permute-start.28 = (bf16[4,48,1536]{2,1,0:T(8,128)(2,1)S(1)}, bf16[4,48,1536]{2,1,0:T(8,128)(2,1)S(1)}, u32[]{:S(2)}, u32[]{:S(2)}) collective-permute-start(bf16[4,48,1536]{2,1,0:T(8,128)(2,1)S(1)} %collective-permute-done.24.refs_2_), channel_id=1, source_target_pairs={{0,2},{1,3},{2,0},{3,1},{4,6},{5,7},{6,4},{7,5},{8,10},{9,11},{10,... | collective-permute-start | bytes 1769480 | tf_op jit(solution)/shard_map/ppermute | solution.py:333
  107.9 25.6 %collective-permute-start.30 = (bf16[2,256,768]{2,1,0:T(8,128)(2,1)S(1)}, bf16[2,256,768]{2,1,0:T(8,128)(2,1)S(1)}, u32[]{:S(2)}, u32[]{:S(2)}) collective-permute-start(bf16[2,256,768]{2,1,0:T(8,128)(2,1)S(1)} %get-tuple-element.510), channel_id=1, source_target_pairs={{0,1},{1,0},{2,3},{3,2},{4,5},{5,4},{6,7},{7,6},{8,9},{9,8},{10,11... | collective-permute-start | bytes 2359304 | tf_op jit(solution)/shard_map/ppermute | solution.py:611
  124.2 9.2 %collective-permute-start.29 = (bf16[4,48,1536]{2,1,0:T(8,128)(2,1)S(1)}, bf16[4,48,1536]{2,1,0:T(8,128)(2,1)S(1)}, u32[]{:S(2)}, u32[]{:S(2)}) collective-permute-start(bf16[4,48,1536]{2,1,0:T(8,128)(2,1)S(1)} %collective-permute-done.25.refs_3_), channel_id=1, source_target_pairs={{0,2},{1,3},{2,0},{3,1},{4,6},{5,7},{6,4},{7,5},{8,10},{9,11},{10,... | collective-permute-start | bytes 1769480 | tf_op jit(solution)/shard_map/ppermute | solution.py:333
  158.8 9.7 %collective-permute-start.32 = (bf16[4,4,48,1536]{3,2,1,0:T(8,128)(2,1)S(1)}, bf16[4,4,48,1536]{3,2,1,0:T(8,128)(2,1)S(1)}, u32[]{:S(2)}, u32[]{:S(2)}) collective-permute-start(bf16[4,4,48,1536]{3,2,1,0:T(8,128)(2,1)S(1)} %get-tuple-element.357), channel_id=1, source_target_pairs={{0,2},{1,3},{2,0},{3,1},{4,6},{5,7},{6,4},{7,5},{8,10},{9,11},{10,... | collective-permute-start | bytes 7077896 | tf_op jit(solution)/shard_map/ppermute | solution.py:333
  158.9 9.6 %collective-permute-start.33 = (bf16[128,768]{1,0:T(8,128)(2,1)S(1)}, bf16[128,768]{1,0:T(8,128)(2,1)S(1)}, u32[]{:S(2)}, u32[]{:S(2)}) collective-permute-start(bf16[128,768]{1,0:T(8,128)(2,1)S(1)} %get-tuple-element.361), channel_id=1, source_target_pairs={{0,1},{1,0},{2,3},{3,2},{4,5},{5,4},{6,7},{7,6},{8,9},{9,8},{10,11... | collective-permute-start | bytes 589832 | tf_op jit(solution)/shard_map/ppermute | solution.py:611
  176.8 22.5 %collective-permute-start.36 = (bf16[4,4,48,1536]{3,2,1,0:T(8,128)(2,1)S(1)}, bf16[4,4,48,1536]{3,2,1,0:T(8,128)(2,1)}, u32[]{:S(2)}, u32[]{:S(2)}) collective-permute-start(bf16[4,4,48,1536]{3,2,1,0:T(8,128)(2,1)S(1)} %get-tuple-element.370), channel_id=1, source_target_pairs={{0,2},{1,3},{2,0},{3,1},{4,6},{5,7},{6,4},{7,5},{8,10},{9,11},{10,... | collective-permute-start | bytes 7077896 | tf_op jit(solution)/shard_map/ppermute | solution.py:333
  178.8 20.4 %collective-permute-start.34 = (bf16[4,48,1536]{2,1,0:T(8,128)(2,1)S(1)}, bf16[4,48,1536]{2,1,0:T(8,128)(2,1)}, u32[]{:S(2)}, u32[]{:S(2)}) collective-permute-start(bf16[4,48,1536]{2,1,0:T(8,128)(2,1)S(1)} %get-tuple-element.501), channel_id=1, source_target_pairs={{0,1},{1,0},{2,6},{3,7},{4,5},{5,4},{6,2},{7,3},{8,9},{9,8},{10,14... | collective-permute-start | bytes 1769480 | tf_op jit(solution)/shard_map/ppermute | solution.py:333
  179.2 20.1 %collective-permute-start.35 = (bf16[4,48,1536]{2,1,0:T(8,128)(2,1)S(1)}, bf16[4,48,1536]{2,1,0:T(8,128)(2,1)}, u32[]{:S(2)}, u32[]{:S(2)}) collective-permute-start(bf16[4,48,1536]{2,1,0:T(8,128)(2,1)S(1)} %get-tuple-element.500), channel_id=1, source_target_pairs={{0,1},{1,0},{2,6},{3,7},{4,5},{5,4},{6,2},{7,3},{8,9},{9,8},{10,14... | collective-permute-start | bytes 1769480 | tf_op jit(solution)/shard_map/ppermute | solution.py:333
  180.9 18.4 %collective-permute-start.37 = (bf16[128,768]{1,0:T(8,128)(2,1)S(1)}, bf16[128,768]{1,0:T(8,128)(2,1)S(1)}, u32[]{:S(2)}, u32[]{:S(2)}) collective-permute-start(bf16[128,768]{1,0:T(8,128)(2,1)S(1)} %get-tuple-element.378), channel_id=1, source_target_pairs={{0,1},{1,0},{2,3},{3,2},{4,5},{5,4},{6,7},{7,6},{8,9},{9,8},{10,11... | collective-permute-start | bytes 589832 | tf_op jit(solution)/shard_map/ppermute | solution.py:611
  202.7 17.1 %collective-permute-start.39 = (bf16[4,48,1536]{2,1,0:T(8,128)(2,1)S(1)}, bf16[4,48,1536]{2,1,0:T(8,128)(2,1)S(1)}, u32[]{:S(2)}, u32[]{:S(2)}) collective-permute-start(bf16[4,48,1536]{2,1,0:T(8,128)(2,1)S(1)} %get-tuple-element.497), channel_id=1, source_target_pairs={{0,1},{1,0},{2,6},{3,7},{4,5},{5,4},{6,2},{7,3},{8,9},{9,8},{10,14... | collective-permute-start | bytes 1769480 | tf_op jit(solution)/shard_map/ppermute | solution.py:333
  203.5 16.4 %collective-permute-start.40 = (bf16[4,4,48,384]{3,2,1,0:T(8,128)(2,1)S(1)}, bf16[4,4,48,384]{3,2,1,0:T(8,128)(2,1)S(1)}, u32[]{:S(2)}, u32[]{:S(2)}) collective-permute-start(bf16[4,4,48,384]{3,2,1,0:T(8,128)(2,1)S(1)} %get-tuple-element.387), channel_id=1, source_target_pairs={{0,2},{1,3},{2,0},{3,1},{4,6},{5,7},{6,4},{7,5},{8,10},{9,11},{10,... | collective-permute-start | bytes 1769480 | tf_op jit(solution)/shard_map/ppermute | solution.py:333
  205.3 15.7 %collective-permute-start.38 = (bf16[4,48,1536]{2,1,0:T(8,128)(2,1)S(1)}, bf16[4,48,1536]{2,1,0:T(8,128)(2,1)S(1)}, u32[]{:S(2)}, u32[]{:S(2)}) collective-permute-start(bf16[4,48,1536]{2,1,0:T(8,128)(2,1)S(1)} %add_convert_fusion.8), channel_id=1, source_target_pairs={{0,4},{1,5},{2,3},{3,2},{4,0},{5,1},{6,7},{7,6},{8,12},{9,13},{10,... | collective-permute-start | bytes 1769480 | tf_op jit(solution)/shard_map/ppermute | solution.py:333
  206.4 42.8 %collective-permute-start.42 = (bf16[4,48,1536]{2,1,0:T(8,128)(2,1)}, bf16[4,48,1536]{2,1,0:T(8,128)(2,1)}, u32[]{:S(2)}, u32[]{:S(2)}) collective-permute-start(bf16[4,48,1536]{2,1,0:T(8,128)(2,1)} %get-tuple-element.496), channel_id=1, source_target_pairs={{0,1},{1,0},{2,6},{3,7},{4,5},{5,4},{6,2},{7,3},{8,9},{9,8},{10,14... | collective-permute-start | bytes 1769480 | tf_op jit(solution)/shard_map/ppermute | solution.py:333
  223.9 25.8 %collective-permute-start.45 = (bf16[256,768]{1,0:T(8,128)(2,1)}, bf16[256,768]{1,0:T(8,128)(2,1)S(1)}, u32[]{:S(2)}, u32[]{:S(2)}) collective-permute-start(bf16[256,768]{1,0:T(8,128)(2,1)} %slice.416), channel_id=1, source_target_pairs={{0,1},{1,0},{2,3},{3,2},{4,5},{5,4},{6,7},{7,6},{8,9},{9,8},{10,11... | collective-permute-start | bytes 1179656 | tf_op jit(solution)/shard_map/ppermute | solution.py:611
  226.4 23.4 %collective-permute-start.43 = (bf16[4,48,384]{2,1,0:T(8,128)(2,1)}, bf16[4,48,384]{2,1,0:T(8,128)(2,1)}, u32[]{:S(2)}, u32[]{:S(2)}) collective-permute-start(bf16[4,48,384]{2,1,0:T(8,128)(2,1)} %get-tuple-element.515), channel_id=1, source_target_pairs={{0,1},{1,0},{2,6},{3,7},{4,5},{5,4},{6,2},{7,3},{8,9},{9,8},{10,14... | collective-permute-start | bytes 442376 | tf_op jit(solution)/shard_map/ppermute | solution.py:333
  226.8 22.9 %collective-permute-start.44 = (bf16[4,48,384]{2,1,0:T(8,128)(2,1)}, bf16[4,48,384]{2,1,0:T(8,128)(2,1)}, u32[]{:S(2)}, u32[]{:S(2)}) collective-permute-start(bf16[4,48,384]{2,1,0:T(8,128)(2,1)} %get-tuple-element.514), channel_id=1, source_target_pairs={{0,1},{1,0},{2,6},{3,7},{4,5},{5,4},{6,2},{7,3},{8,9},{9,8},{10,14... | collective-permute-start | bytes 442376 | tf_op jit(solution)/shard_map/ppermute | solution.py:333
  230.5 19.2 %collective-permute-start.41 = (bf16[2,48,1536]{2,1,0:T(8,128)(2,1)}, bf16[2,48,1536]{2,1,0:T(8,128)(2,1)}, u32[]{:S(2)}, u32[]{:S(2)}) collective-permute-start(bf16[2,48,1536]{2,1,0:T(8,128)(2,1)} %get-tuple-element.524), channel_id=1, source_target_pairs={{0,16},{1,17},{2,18},{3,19},{4,20},{5,21},{6,22},{7,23},{8,24},{9,... | collective-permute-start | bytes 884744 | tf_op jit(solution)/shard_map/ppermute | solution.py:333
  249.3 12.0 %collective-permute-start.46 = (bf16[128,768]{1,0:T(8,128)(2,1)}, bf16[128,768]{1,0:T(8,128)(2,1)S(1)}, u32[]{:S(2)}, u32[]{:S(2)}) collective-permute-start(bf16[128,768]{1,0:T(8,128)(2,1)} %get-tuple-element.409), channel_id=1, source_target_pairs={{0,1},{1,0},{2,3},{3,2},{4,5},{5,4},{6,7},{7,6},{8,9},{9,8},{10,11... | collective-permute-start | bytes 589832 | tf_op jit(solution)/shard_map/ppermute | solution.py:611
  251.4 25.7 %collective-permute-start.53 = (bf16[4,48,384]{2,1,0:T(8,128)(2,1)}, bf16[4,48,384]{2,1,0:T(8,128)(2,1)}, u32[]{:S(2)}, u32[]{:S(2)}) collective-permute-start(bf16[4,48,384]{2,1,0:T(8,128)(2,1)} %add_convert_fusion.22), channel_id=1, source_target_pairs={{0,4},{1,5},{2,3},{3,2},{4,0},{5,1},{6,7},{7,6},{8,12},{9,13},{10,... | collective-permute-start | bytes 442376 | tf_op jit(solution)/shard_map/ppermute | solution.py:333
  254.3 9.9 %collective-permute-start.47 = (bf16[4,48,1536]{2,1,0:T(8,128)(2,1)S(1)}, bf16[4,48,1536]{2,1,0:T(8,128)(2,1)S(1)}, u32[]{:S(2)}, u32[]{:S(2)}) collective-permute-start(bf16[4,48,1536]{2,1,0:T(8,128)(2,1)S(1)} %add_convert_fusion.2), channel_id=1, source_target_pairs={{0,4},{1,5},{2,3},{3,2},{4,0},{5,1},{6,7},{7,6},{8,12},{9,13},{10,... | collective-permute-start | bytes 1769480 | tf_op jit(solution)/shard_map/ppermute | solution.py:333
  271.3 16.9 %collective-permute-start.52 = (bf16[2,48,1536]{2,1,0:T(8,128)(2,1)}, bf16[2,48,1536]{2,1,0:T(8,128)(2,1)}, u32[]{:S(2)}, u32[]{:S(2)}) collective-permute-start(bf16[2,48,1536]{2,1,0:T(8,128)(2,1)} %get-tuple-element.522), channel_id=1, source_target_pairs={{0,16},{1,17},{2,18},{3,19},{4,20},{5,21},{6,22},{7,23},{8,24},{9,... | collective-permute-start | bytes 884744 | tf_op jit(solution)/shard_map/ppermute | solution.py:333
  274.2 14.0 %collective-permute-start.49 = (bf16[4,160,384]{2,1,0:T(8,128)(2,1)}, bf16[4,160,384]{2,1,0:T(8,128)(2,1)}, u32[]{:S(2)}, u32[]{:S(2)}) collective-permute-start(bf16[4,160,384]{2,1,0:T(8,128)(2,1)} %get-tuple-element.505), channel_id=1, source_target_pairs={{0,1},{1,0},{2,6},{3,7},{4,5},{5,4},{6,2},{7,3},{8,9},{9,8},{10,14... | collective-permute-start | bytes 1474568 | tf_op jit(solution)/shard_map/ppermute | solution.py:333
  274.9 13.7 %collective-permute-start.50 = (bf16[4,160,384]{2,1,0:T(8,128)(2,1)}, bf16[4,160,384]{2,1,0:T(8,128)(2,1)}, u32[]{:S(2)}, u32[]{:S(2)}) collective-permute-start(bf16[4,160,384]{2,1,0:T(8,128)(2,1)} %get-tuple-element.504), channel_id=1, source_target_pairs={{0,1},{1,0},{2,6},{3,7},{4,5},{5,4},{6,2},{7,3},{8,9},{9,8},{10,14... | collective-permute-start | bytes 1474568 | tf_op jit(solution)/shard_map/ppermute | solution.py:333
  304.0 10.2 %collective-permute-start.61 = (bf16[48,384]{1,0:T(8,128)(2,1)S(1)}, bf16[48,384]{1,0:T(8,128)(2,1)S(1)}, u32[]{:S(2)}, u32[]{:S(2)}) collective-permute-start(bf16[48,384]{1,0:T(8,128)(2,1)S(1)} %slice_bitcast_fusion.17), channel_id=1, source_target_pairs={{0,8},{1,9},{2,10},{3,11},{4,12},{5,13},{6,14},{7,15},{8,0},{9,1},... | collective-permute-start | bytes 110600 | tf_op jit(solution)/shard_map/ppermute | solution.py:333
  304.6 10.3 %collective-permute-start.60 = (bf16[256,768]{1,0:T(8,128)(2,1)S(1)}, bf16[256,768]{1,0:T(8,128)(2,1)S(1)}, u32[]{:S(2)}, u32[]{:S(2)}) collective-permute-start(bf16[256,768]{1,0:T(8,128)(2,1)S(1)} %copy-done.57), channel_id=1, source_target_pairs={{0,1},{1,0},{2,3},{3,2},{4,5},{5,4},{6,7},{7,6},{8,9},{9,8},{10,11... | collective-permute-start | bytes 1179656 | tf_op jit(solution)/shard_map/ppermute | solution.py:611
  306.7 10.7 %collective-permute-start.57 = (bf16[160,384]{1,0:T(8,128)(2,1)S(1)}, bf16[160,384]{1,0:T(8,128)(2,1)S(1)}, u32[]{:S(2)}, u32[]{:S(2)}) collective-permute-start(bf16[160,384]{1,0:T(8,128)(2,1)S(1)} %get-tuple-element.528), channel_id=1, source_target_pairs={{0,8},{1,9},{2,10},{3,11},{4,12},{5,13},{6,14},{7,15},{8,0},{9,1},... | collective-permute-start | bytes 368648 | tf_op jit(solution)/shard_map/ppermute | solution.py:333
  308.7 9.4 %collective-permute-start.58 = (bf16[160,384]{1,0:T(8,128)(2,1)S(1)}, bf16[160,384]{1,0:T(8,128)(2,1)S(1)}, u32[]{:S(2)}, u32[]{:S(2)}) collective-permute-start(bf16[160,384]{1,0:T(8,128)(2,1)S(1)} %get-tuple-element.527), channel_id=1, source_target_pairs={{0,16},{1,17},{2,18},{3,19},{4,20},{5,21},{6,22},{7,23},{8,24},{9,... | collective-permute-start | bytes 368648 | tf_op jit(solution)/shard_map/ppermute | solution.py:333
  (89 other events, 603.1 us)
